TPU v7x, 32 devices: a whole 2x2x4 slice. The times are simulated.
32 devices in a mesh: ctx: 8 (over z, y), fsdp: 4 (over x, core).
Axes of the slice: x: 2, y: 2, z: 4, core: 2. Of those that a mesh axis runs over, the one named last changes fastest.
Arguments:
- tokens: bfloat16 [4, 2048, 768], P('fsdp', 'ctx'), may hold values from -6 to 6
- encoded: bfloat16 [4, 1024, 768], P('fsdp', 'ctx'), may hold values from -6 to 6
- cotangent: bfloat16 [4, 2048, 768], P('fsdp', 'ctx'), may hold values from -6 to 6
- w_self: bfloat16 [768, 3072], P('fsdp'), may hold values from -1 to 1
- w_cross: bfloat16 [768, 3072], P('fsdp'), may hold values from -1 to 1
- w_ffn: bfloat16 [768, 6144], P('fsdp'), may hold values from -1 to 1
- gains: bfloat16 [3, 768], P(None, 'fsdp'), may hold values from 0.5 to 1.5
- table: bfloat16 [32, 12], P('fsdp'), may hold values from -4 to 4
- bucket_ids: int32 [2048], replicated, may hold values from 0 to 31, as said below
- block_order: int32 [16], replicated, may hold values from 0 to 15, each once
Outputs:
- output: bfloat16 [4, 2048, 768], P('fsdp', 'ctx')
- grad_tokens: bfloat16 [4, 2048, 768], P('fsdp', 'ctx')
- grad_encoded: bfloat16 [4, 1024, 768], P('fsdp', 'ctx')
- grad_w_self: float32 [768, 3072], P('fsdp')
- grad_w_cross: float32 [768, 3072], P('fsdp')
- feedforward_weight_gradient: float32 [768, 6144], P('fsdp')
- grad_gains: float32 [3, 768], P(None, 'fsdp')
- grad_table: float32 [32, 12], P('fsdp')
Inputs may be any that keep to these rules, and one draw needn't show every extreme that they name: `bucket_ids`: nondecreasing in the distance; distances 0 to 7 have buckets 0 to 7, and the buckets above grow about logarithmically with the distance. Each block number once; ctx device c holds block block_order[2 * c] in its first 128 rows and block_order[2 * c + 1] in the rest.
All inputs are finite; a program needn't handle non-finite values.
Results may differ from a plain program's by a relative error of at most 0.04.
Values may be sent and summed in bfloat16 or wider, within the bound.
No kernel may reach another device: no remote copies, remote signals or barrier semaphores. Data moves between devices by JAX's collectives and lax.ppermute only.
A program may use at most 192 MiB of HBM per device.

v0:
```python
import math

import jax
import jax.numpy as jnp
from jax import lax
from jax.sharding import PartitionSpec as P

EPSILON = 1e-06
NEGATIVE = -1e30


def row_norm(values, gain):
    return values * lax.rsqrt(jnp.mean(values * values, axis=-1, keepdims=True) + EPSILON) * gain


def times_transposed(left, right):
    return lax.dot_general(
        left, right, (((1,), (1,)), ((), ())), preferred_element_type=jnp.float32
    )


def transposed_times(left, right):
    return lax.dot_general(
        left, right, (((0,), (0,)), ((), ())), preferred_element_type=jnp.float32
    )


def to_heads(matrix, head_count):
    return jnp.transpose(
        matrix.reshape(matrix.shape[0], head_count, matrix.shape[1] // head_count), (1, 0, 2)
    )


def from_heads(stacked):
    return jnp.transpose(stacked, (1, 0, 2)).reshape(
        stacked.shape[1], stacked.shape[0] * stacked.shape[2]
    )


def positions(block_order, first_row, row_total, half_rows):
    global_rows = first_row + jnp.arange(row_total, dtype=jnp.int32)
    matches = (global_rows // half_rows)[:, None] == jnp.arange(
        block_order.shape[0], dtype=jnp.int32
    )[None, :]
    return (
        jnp.sum(jnp.where(matches, block_order[None, :], 0), axis=1) * half_rows
        + global_rows % half_rows
    )


def in_blocks(step_fn, carry_state, key_piece, block_size):
    block_size = math.gcd(key_piece.shape[0], block_size)

    def advance(step_index, current):
        offset_rows = step_index * block_size
        return step_fn(
            current, lax.dynamic_slice_in_dim(key_piece, offset_rows, block_size, 0), offset_rows
        )

    return lax.fori_loop(0, key_piece.shape[0] // block_size, advance, carry_state)


def cross_forward(operands):
    query_rows, key_rows, value_rows = operands
    probabilities = jax.nn.softmax(times_transposed(query_rows, key_rows), axis=-1)
    return jnp.dot(
        probabilities.astype(jnp.bfloat16), value_rows, preferred_element_type=jnp.float32
    )


def cross_attention_backward(operands):
    query_rows, key_rows, value_rows, grad_rows = operands
    probabilities = jax.nn.softmax(times_transposed(query_rows, key_rows), axis=-1)
    grad_probs = times_transposed(grad_rows, value_rows)
    score_gradient = (
        probabilities * (grad_probs - jnp.sum(probabilities * grad_probs, axis=-1, keepdims=True))
    ).astype(jnp.bfloat16)
    grad_query = jnp.dot(score_gradient, key_rows, preferred_element_type=jnp.float32)
    grad_key = transposed_times(score_gradient, query_rows)
    grad_value = transposed_times(probabilities.astype(jnp.bfloat16), grad_rows)
    return (grad_query, grad_key, grad_value)


def gated_gelu(gate_up):
    hidden_units = gate_up.shape[1] // 2
    return jax.nn.gelu(gate_up[:, :hidden_units], approximate=True) * gate_up[:, hidden_units:]


def body(tokens, encoded, cotangent, w_self, w_cross, w_ffn, gains, table, bucket_ids, block_order):
    row_count = tokens.shape[1]
    model_width = tokens.shape[2]
    head_count = table.shape[1]
    head_size = model_width // head_count
    hidden_units = w_ffn.shape[1] // 3
    half_rows = row_count // 2
    seq_length = bucket_ids.shape[0]
    ctx_place = lax.axis_index("ctx")
    whole_self, gain_rows, bias_table_rows = (
        lax.all_gather(w_self, "fsdp", axis=0, tiled=True),
        lax.all_gather(gains, "fsdp", axis=1, tiled=True),
        lax.all_gather(table, "fsdp", axis=0, tiled=True),
    )
    whole_cross = lax.all_gather(w_cross, "fsdp", axis=0, tiled=True)
    whole_ffn = lax.all_gather(w_ffn, "fsdp", axis=0, tiled=True)
    bucket_count = bias_table_rows.shape[0]
    gain_float = gain_rows.astype(jnp.float32)
    inputs = tokens[0].astype(jnp.float32)
    encoder_rows = encoded[0]
    query_pos = positions(block_order, ctx_place * row_count, row_count, half_rows)
    bucket_range = jnp.arange(bucket_count, dtype=jnp.int32)
    bucket_starts = jnp.sum((bucket_ids[:, None] < bucket_range[None, :]).astype(jnp.int32), axis=0)
    normed_one = row_norm(inputs, gain_float[0]).astype(jnp.bfloat16)
    projected = jnp.dot(
        normed_one, whole_self[:, : 3 * model_width], preferred_element_type=jnp.float32
    ).astype(jnp.bfloat16)
    query_heads = to_heads(projected[:, :model_width], head_count)
    key_values = projected[:, model_width:]

    def score_piece(key_block, first_row):
        block_rows = key_block.shape[0]
        key_heads = key_block[:, :model_width].reshape(block_rows, head_count, head_size)
        value_heads = key_block[:, model_width:].reshape(block_rows, head_count, head_size)
        key_pos = positions(block_order, first_row, block_rows, half_rows)
        offsets = query_pos[:, None] - key_pos[None, :]
        reached = (offsets[None] >= bucket_starts[:, None, None]).astype(jnp.bfloat16)
        bucket_match_counts = reached - jnp.concatenate(
            [reached[1:], jnp.zeros_like(reached[:1])], axis=0
        )
        extra = jnp.einsum(
            "vei,vy->yei", bucket_match_counts, bias_table_rows, preferred_element_type=jnp.float32
        )
        scores = (
            jnp.einsum("hqd,khd->hqk", query_heads, key_heads, preferred_element_type=jnp.float32)
            + extra
        )
        return (
            jnp.where((offsets >= 0)[None], scores, NEGATIVE),
            bucket_match_counts,
            key_heads,
            value_heads,
        )

    def forward_step(current, key_block, first_row):
        running_max, running_sum, running_out = current
        scores, bucket_match_counts, key_heads, value_heads = score_piece(key_block, first_row)
        newest = jnp.maximum(running_max, jnp.max(scores, axis=-1))
        rescale = jnp.exp(running_max - newest)
        weights = jnp.exp(scores - newest[..., None])
        running_sum = running_sum * rescale + jnp.sum(weights, axis=-1)
        running_out = running_out * rescale[..., None] + jnp.einsum(
            "hqk,khd->hqd",
            weights.astype(jnp.bfloat16),
            value_heads,
            preferred_element_type=jnp.float32,
        )
        return (newest, running_sum, running_out)

    start_state = (
        jnp.full((head_count, row_count), NEGATIVE, jnp.float32),
        jnp.zeros((head_count, row_count), jnp.float32),
        jnp.zeros((head_count, row_count, head_size), jnp.float32),
    )
    running_max, running_sum, running_out = in_blocks(
        forward_step, start_state, lax.all_gather(key_values, "ctx", axis=0, tiled=True), row_count
    )
    attended = running_out / running_sum[..., None]
    log_total = running_max + jnp.log(running_sum)
    attended_rows = from_heads(attended).astype(jnp.bfloat16)
    after_one = inputs + jnp.dot(
        attended_rows, whole_self[:, 3 * model_width :], preferred_element_type=jnp.float32
    )
    normed_two = row_norm(after_one, gain_float[1]).astype(jnp.bfloat16)
    cross_query = jnp.dot(
        normed_two, whole_cross[:, :model_width], preferred_element_type=jnp.float32
    ).astype(jnp.bfloat16)
    encoder_local = jnp.dot(
        encoder_rows,
        whole_cross[:, model_width : 3 * model_width],
        preferred_element_type=jnp.float32,
    ).astype(jnp.bfloat16)
    encoder_kv = lax.all_gather(encoder_local, "ctx", axis=0, tiled=True)
    cross_heads = to_heads(cross_query, head_count)
    cross_keys = to_heads(encoder_kv[:, :model_width], head_count)
    cross_values = to_heads(encoder_kv[:, model_width:], head_count)
    cross_rows = from_heads(lax.map(cross_forward, (cross_heads, cross_keys, cross_values))).astype(
        jnp.bfloat16
    )
    after_two = after_one + jnp.dot(
        cross_rows, whole_cross[:, 3 * model_width :], preferred_element_type=jnp.float32
    )
    normed_three = row_norm(after_two, gain_float[2]).astype(jnp.bfloat16)
    gate_up = jnp.dot(
        normed_three, whole_ffn[:, : 2 * hidden_units], preferred_element_type=jnp.float32
    )
    mixed_float, gated_back = jax.vjp(gated_gelu, gate_up)
    mixed_rows = mixed_float.astype(jnp.bfloat16)
    output = (after_two + times_transposed(mixed_rows, whole_ffn[:, 2 * hidden_units :])).astype(
        jnp.bfloat16
    )
    grad_after_two = cotangent[0].astype(jnp.float32)
    grad_branch_three = grad_after_two.astype(jnp.bfloat16)
    grad_mixed = jnp.dot(
        grad_branch_three, whole_ffn[:, 2 * hidden_units :], preferred_element_type=jnp.float32
    )
    grad_gate_up = gated_back(grad_mixed)[0].astype(jnp.bfloat16)
    grad_normed_three = times_transposed(grad_gate_up, whole_ffn[:, : 2 * hidden_units])
    upper = transposed_times(normed_three, grad_gate_up)
    lower = transposed_times(grad_branch_three, mixed_rows)
    ffn_grad = lax.psum_scatter(
        jnp.concatenate([upper, lower], axis=1).astype(jnp.bfloat16),
        "fsdp",
        scatter_dimension=0,
        tiled=True,
    )
    norm_back = jax.vjp(row_norm, after_two, gain_float[2])[1]
    norm_part, gain_three = norm_back(grad_normed_three)
    grad_after_one = grad_after_two + norm_part
    grad_branch_two = grad_after_one.astype(jnp.bfloat16)
    grad_cross_rows = times_transposed(grad_branch_two, whole_cross[:, 3 * model_width :]).astype(
        jnp.bfloat16
    )
    grad_cq, grad_ck, grad_cv = lax.map(
        cross_attention_backward,
        (cross_heads, cross_keys, cross_values, to_heads(grad_cross_rows, head_count)),
    )
    grad_cross_query = from_heads(grad_cq).astype(jnp.bfloat16)
    encoder_full = jnp.concatenate([from_heads(grad_ck), from_heads(grad_cv)], axis=1)
    grad_encoder_kv = lax.psum_scatter(
        encoder_full.astype(jnp.bfloat16), "ctx", scatter_dimension=0, tiled=True
    )
    grad_encoded = times_transposed(
        grad_encoder_kv, whole_cross[:, model_width : 3 * model_width]
    ).astype(jnp.bfloat16)
    grad_normed_two = times_transposed(grad_cross_query, whole_cross[:, :model_width])
    query_part = transposed_times(normed_two, grad_cross_query)
    encoder_part = transposed_times(encoder_rows, grad_encoder_kv)
    output_slice = transposed_times(cross_rows, grad_branch_two)
    cross_grad = lax.psum_scatter(
        jnp.concatenate([query_part, encoder_part, output_slice], axis=1).astype(jnp.bfloat16),
        "fsdp",
        scatter_dimension=0,
        tiled=True,
    )
    norm_back = jax.vjp(row_norm, after_one, gain_float[1])[1]
    norm_part, gain_two = norm_back(grad_normed_two)
    grad_inputs_one = grad_after_one + norm_part
    grad_branch_one = grad_inputs_one.astype(jnp.bfloat16)
    grad_heads = to_heads(
        times_transposed(grad_branch_one, whole_self[:, 3 * model_width :]).astype(jnp.bfloat16),
        head_count,
    )
    delta = jnp.sum(grad_heads.astype(jnp.float32) * attended, axis=-1)

    def backward_step(current, key_block, first_row):
        grad_query, grad_keys, grad_table = current
        block_rows = key_block.shape[0]
        scores, bucket_match_counts, key_heads, value_heads = score_piece(key_block, first_row)
        probabilities = jnp.exp(scores - log_total[..., None])
        grad_probs = jnp.einsum(
            "hqd,khd->hqk", grad_heads, value_heads, preferred_element_type=jnp.float32
        )
        score_gradient = (probabilities * (grad_probs - delta[..., None])).astype(jnp.bfloat16)
        grad_query = grad_query + jnp.einsum(
            "hqk,khd->hqd", score_gradient, key_heads, preferred_element_type=jnp.float32
        )
        grad_key_rows = jnp.einsum(
            "hqk,hqd->khd", score_gradient, query_heads, preferred_element_type=jnp.float32
        ).reshape(block_rows, model_width)
        grad_value_rows = jnp.einsum(
            "hqk,hqd->khd",
            probabilities.astype(jnp.bfloat16),
            grad_heads,
            preferred_element_type=jnp.float32,
        ).reshape(block_rows, model_width)
        grad_table = grad_table + jnp.einsum(
            "cfg,xfg->xc", score_gradient, bucket_match_counts, preferred_element_type=jnp.float32
        )
        current_rows = lax.dynamic_slice_in_dim(grad_keys, first_row, block_rows, 0)
        updated = current_rows + jnp.concatenate([grad_key_rows, grad_value_rows], axis=1)
        grad_keys = lax.dynamic_update_slice_in_dim(grad_keys, updated, first_row, 0)
        return (grad_query, grad_keys, grad_table)

    back_state = (
        jnp.zeros((head_count, row_count, head_size), jnp.float32),
        jnp.zeros((seq_length, 2 * model_width), jnp.float32),
        jnp.zeros((bucket_count, head_count), jnp.float32),
    )
    grad_query, grad_key_full, grad_table = in_blocks(
        backward_step, back_state, lax.all_gather(key_values, "ctx", axis=0, tiled=True), row_count
    )
    grad_key_own = lax.psum_scatter(
        grad_key_full.astype(jnp.bfloat16), "ctx", scatter_dimension=0, tiled=True
    )
    grad_projected = jnp.concatenate(
        [from_heads(grad_query).astype(jnp.bfloat16), grad_key_own], axis=1
    )
    grad_normed_one = times_transposed(grad_projected, whole_self[:, : 3 * model_width])
    input_part = transposed_times(normed_one, grad_projected)
    output_slice = transposed_times(attended_rows, grad_branch_one)
    self_grad = lax.psum_scatter(
        jnp.concatenate([input_part, output_slice], axis=1).astype(jnp.bfloat16),
        "fsdp",
        scatter_dimension=0,
        tiled=True,
    )
    norm_back = jax.vjp(row_norm, inputs, gain_float[0])[1]
    norm_part, first_norm_gain = norm_back(grad_normed_one)
    grad_tokens = (grad_inputs_one + norm_part).astype(jnp.bfloat16)
    gain_terms = jnp.stack([first_norm_gain, gain_two, gain_three])
    gain_share, table_share = (
        lax.psum_scatter(gain_terms, "fsdp", scatter_dimension=1, tiled=True),
        lax.psum_scatter(grad_table, "fsdp", scatter_dimension=0, tiled=True),
    )
    totals = (
        lax.psum(self_grad, "ctx").astype(jnp.float32),
        lax.psum(cross_grad, "ctx").astype(jnp.float32),
        lax.psum(ffn_grad, "ctx").astype(jnp.float32),
        lax.psum(gain_share.astype(jnp.bfloat16), "ctx").astype(jnp.float32),
        lax.psum(table_share.astype(jnp.bfloat16), "ctx").astype(jnp.float32),
    )
    return (
        output[None],
        grad_tokens[None],
        grad_encoded[None],
        totals[0],
        totals[1],
        totals[2],
        totals[3],
        totals[4],
    )


def solution(mesh):
    in_specs = (
        P("fsdp", "ctx", None),
        P("fsdp", "ctx", None),
        P("fsdp", "ctx", None),
        P("fsdp", None),
        P("fsdp", None),
        P("fsdp", None),
        P(None, "fsdp"),
        P("fsdp", None),
        P(),
        P(),
    )
    out_specs = (
        P("fsdp", "ctx", None),
        P("fsdp", "ctx", None),
        P("fsdp", "ctx", None),
        P("fsdp", None),
        P("fsdp", None),
        P("fsdp", None),
        P(None, "fsdp"),
        P("fsdp", None),
    )
    return jax.shard_map(body, mesh=mesh, in_specs=in_specs, out_specs=out_specs, check_vma=False)
```

profile of v0, /device:TPU:0, one launch (start us, length us, event | category | flops | bytes accessed | tf_op | source)
XLA Modules:
  0.0 1377.2 jit_solution(8934288994584734069)
XLA Ops:
  8.7 41.1 %all-gather.11.cloned.1.call-done = bf16[768,3072]{1,0:T(8,128)(2,1)} async-done(((bf16[192,3072]{1,0:T(8,128)(2,1)}), bf16[768,3072]{1,0:T(8,128)(2,1)}) %all-gather.11.cloned.1.call-update) | async-done | bytes 4718608 | tf_op jit(solution)/shard_map/all_gather | solution.py:103
  52.8 5.2 all-gather
  58.3 30.5 %all-gather.7.cloned.1.call-done = bf16[768,3072]{1,0:T(8,128)(2,1)} async-done(((bf16[192,3072]{1,0:T(8,128)(2,1)}), bf16[768,3072]{1,0:T(8,128)(2,1)}) %all-gather.7.cloned.1.call-update) | async-done | bytes 4718608 | tf_op jit(solution)/shard_map/all_gather | solution.py:99
  94.0 5.2 all_gather.25
  100.2 51.9 %all-gather.13.cloned.1.call-done = bf16[1024,1536]{1,0:T(8,128)(2,1)} async-done(((bf16[128,1536]{1,0:T(8,128)(2,1)}), bf16[1024,1536]{1,0:T(8,128)(2,1)}) %all-gather.13.cloned.1.call-update) | async-done | bytes 3145744 | tf_op jit(solution)/shard_map/all_gather | solution.py:181
  164.0 88.4 %all-gather.9.cloned.1.call-done = bf16[2048,1536]{1,0:T(8,128)(2,1)} async-done(((bf16[256,1536]{1,0:T(8,128)(2,1)}), bf16[2048,1536]{1,0:T(8,128)(2,1)}) %all-gather.9.cloned.1.call-update) | async-done | bytes 6291472 | tf_op jit(solution)/shard_map/all_gather | solution.py:164
  252.4 8.9 copy.143
  261.3 148.1 %while.66 = (s32[]{:T(128)}, f32[12,256]{1,0:T(8,128)S(1)}, f32[12,256]{1,0:T(8,128)S(1)}, f32[12,256,64]{1,2,0:T(8,128)}, s32[256]{0:T(256)S(1)}, /*index=5*/s3...) while((s32[]{:T(128)}, f32[12,256]{1,0:T(8,128)S(1)}, ...), condition=%wide.region_7.8_spmd.clone, body=%wide.region_3.7_spmd.clone.sunk | while | flops 274761984 | bytes 52242808 | solution.py:60
  415.4 36.3 %while.64 = (s32[]{:T(128)}, bf16[12,256,64]{1,2,0:T(8,128)(2,1)S(1)}, bf16[12,256,64]{2,1,0:T(8,128)(2,1)S(1)}, bf16[12,1024,64]{2,1,0:T(8,128)(2,1)}, bf16[12,1024,64]{2,1,0:T(8,128)(2,1)}, /*index=5*/s32[]{:T(128)}) while((s32[]{:T(128)}, bf16[12,256,64]{1,2,0:T(8,128)(2,1)S(1)}, bf16[12,256,64]{2,1,0:T(8,128)(2,1)S(1)}, ...), condition=%wide.region_12.13_spmd, body=%wide.region_9.12_spmd.sunk | while | flops 68681216 | bytes 3808333 | solution.py:185
  453.7 4.9 fusion.74
  468.5 79.6 %while.65 = (s32[]{:T(128)}, bf16[12,256,64]{1,2,0:T(8,128)(2,1)S(1)}, bf16[12,1024,64]{1,2,0:T(8,128)(2,1)}, bf16[12,1024,64]{1,2,0:T(8,128)(2,1)}, bf16[12,256...) while((s32[]{:T(128)}, ...), condition=%wide.region_19.20_spmd, body=%wide.region_15.19_spmd.sunk | while | flops 171703552 | bytes 10502245 | solution.py:222
  560.4 6.1 broadcast_in_dim.254
  566.6 279.3 %while.67 = (s32[]{:T(128)}, f32[12,256,64]{1,2,0:T(8,128)}, f32[2048,1536]{0,1:T(8,128)}, f32[32,12]{0,1:T(8,128)S(1)}, s32[256]{0:T(256)S(1)}, /*index=5*/s32[...) while((s32[]{:T(128)}, f32[12,256,64]{1,2,0:T(8,128)}, ...), condition=%wide.region_24.25_spmd.clone, body=%wide.region_22.24_spmd.clone.sunk | while | flops 640241664 | bytes 101488384 | solution.py:60
  594.3 4.5 fusion.277
  629.3 4.5 fusion.277
  664.1 4.5 fusion.277
  699.0 4.5 fusion.277
  733.9 4.5 fusion.277
  768.7 4.5 fusion.277
  803.6 4.5 fusion.277
  838.4 4.5 fusion.277
  845.8 8.2 convert_element_type.218
  862.8 6.6 copy.171
  875.2 4.2 pad_maximum_fusion
  882.7 88.1 %reduce-scatter.13.cloned.1.call-done = bf16[256,1536]{0,1:T(8,128)(2,1)} async-done(((bf16[2048,1536]{0,1:T(8,128)(2,1)}), bf16[256,1536]{0,1:T(8,128)(2,1)}) %reduce-scatter.13.cloned.1.call-update) | async-done | bytes 786448 | tf_op jit(solution)/shard_map/reduce_scatter | solution.py:291
  977.3 4.8 fusion.119
  983.1 37.3 %reduce-scatter.21.cloned.1.call-done = bf16[192,3072]{1,0:T(8,128)(2,1)} async-done(((bf16[768,3072]{1,0:T(8,128)(2,1)}), bf16[192,3072]{1,0:T(8,128)(2,1)}) %reduce-scatter.21.cloned.1.call-update) | async-done | bytes 1179664
  1022.9 78.7 %reduce-scatter.17.cloned.1.call-done = bf16[192,6144]{1,0:T(8,128)(2,1)} async-done(((bf16[768,6144]{1,0:T(8,128)(2,1)}), bf16[192,6144]{1,0:T(8,128)(2,1)}) %reduce-scatter.17.cloned.1.call-update) | async-done | bytes 2359312 | tf_op jit(solution)/shard_map/reduce_scatter | solution.py:209
  1101.6 51.0 %reduce-scatter.15.cloned.1.call-done = bf16[192,3072]{1,0:T(8,128)(2,1)} async-done(((bf16[768,3072]{1,0:T(8,128)(2,1)}), bf16[192,3072]{1,0:T(8,128)(2,1)}) %reduce-scatter.15.cloned.1.call-update) | async-done | bytes 1179664 | tf_op jit(solution)/shard_map/reduce_scatter | solution.py:300
  1154.0 10.1 all-reduce.4
  1177.0 21.9 %all-reduce.5 = (bf16[3,192]{1,0:T(4,128)(2,1)S(1)}, bf16[8,12]{1,0:T(8,128)(2,1)S(1)}) all-reduce(bf16[3,192]{1,0:T(4,128)(2,1)S(1)} %copy.174, bf16[8,12]{1,0:T(8,128)(2,1)S(1)} %dynamic-slice_convert_fusion), channel_id=1, replica_groups=mesh['ctx'=8,'fsdp'=4] {'ctx'}, use_global_device_ids=true, to_apply=%region_38.39 | all-reduce | flops 672 | bytes 2688 | tf_op jit(solution)/shard_map/psum | solution.py:318
  1200.1 161.3 %all-reduce.9.cloned.1.call-done = (bf16[192,3072]{0,1:T(8,128)(2,1)}, bf16[192,3072]{1,0:T(8,128)(2,1)}, bf16[192,6144]{1,0:T(8,128)(2,1)}) async-done(((bf16[192,3072]{0,1:T(8,128)(2,1)}, bf16[192,3072]{1,0:T(8,128)(2,1)}, bf16[192,6144]{1,0:T(8,128)(2,1)}), (bf16[192,3072]{0,1:T(8,128)(2,1)}, bf16[192,3072]{1,0:T(8,128)(2,1)}, bf16[192,6144]{1,0:T(8,128)(2,1)})) %all-reduce.9.cloned.1.call-update) | async-done | bytes 4718608 | tf_op jit(solution)/shard_map/psum | solution.py:316
  (834 shorter events, 608.0 us)
Async XLA Ops:
  7.2 42.6 %copy-start = (bf16[1,128,768]{2,1,0:T(8,128)(2,1)S(1)}, bf16[1,128,768]{2,1,0:T(8,128)(2,1)}, u32[]{:S(2)}) copy-start(bf16[1,128,768]{2,1,0:T(8,128)(2,1)} %param.19) | copy-start | bytes 589828
  7.2 45.6 %copy-start.61 = (bf16[3,192]{1,0:T(4,128)(2,1)S(1)}, bf16[3,192]{1,0:T(4,128)(2,1)}, u32[]{:S(2)}) copy-start(bf16[3,192]{1,0:T(4,128)(2,1)} %param.24) | copy-start | bytes 3460
  7.2 50.9 %copy-start.29 = (bf16[1,256,768]{2,1,0:T(8,128)(2,1)S(1)}, bf16[1,256,768]{2,1,0:T(8,128)(2,1)}, u32[]{:S(2)}) copy-start(bf16[1,256,768]{2,1,0:T(8,128)(2,1)} %param.18) | copy-start | bytes 1179652
  7.2 42.6 %all-gather.11.cloned.1.call-start = ((), (), s32[]{:S(2)}) async-start(), calls=%async_computation.8 | async-start | bytes 5898240 | tf_op jit(solution)/shard_map/all_gather | solution.py:103
  7.9 80.9 %all-gather.7.cloned.1.call-start = ((), (), s32[]{:S(2)}) async-start(), calls=%async_computation.6 | async-start | bytes 5898240 | tf_op jit(solution)/shard_map/all_gather | solution.py:99
  8.7 143.4 %all-gather.13.cloned.1.call-start = ((), (), s32[]{:S(2)}) async-start(), calls=%async_computation.9 | async-start | bytes 3538944 | tf_op jit(solution)/shard_map/all_gather | solution.py:181
  52.7 199.7 %all-gather.9.cloned.1.call-start = ((), (), s32[]{:S(2)}) async-start(), calls=%async_computation.7 | async-start | bytes 7077888 | tf_op jit(solution)/shard_map/all_gather | solution.py:164
  58.1 33.9 %copy-start.48 = (f32[768]{0:T(1024)}, f32[768]{0:T(1024)S(1)}, u32[]{:S(2)}) copy-start(f32[768]{0:T(1024)S(1)} %get-tuple-element.939) | copy-start | bytes 9220
  58.1 407.3 %copy-start.50 = (f32[768]{0:T(1024)}, f32[768]{0:T(1024)S(1)}, u32[]{:S(2)}) copy-start(f32[768]{0:T(1024)S(1)} %get-tuple-element.937) | copy-start | bytes 9220
  58.3 30.6 %copy-start.57 = (f32[256]{0:T(256)}, f32[256]{0:T(256)S(1)}, u32[]{:S(2)}) copy-start(f32[256]{0:T(256)S(1)} %fusion.124) | copy-start | bytes 3076
  58.3 30.6 %copy-start.53 = (f32[256]{0:T(256)}, f32[256]{0:T(256)S(1)}, u32[]{:S(2)}) copy-start(f32[256]{0:T(256)S(1)} %fusion.141) | copy-start | bytes 3076
  93.0 360.7 %all-gather.15.cloned.1.call-start = ((), (), s32[]{:S(2)}) async-start(), calls=%async_computation.10 | async-start | bytes 11796480 | tf_op jit(solution)/shard_map/all_gather | solution.py:104
  93.6 764.8 %reduce-scatter.19.cloned.1.call-start = ((), (), s32[]{:S(2)}) async-start(), calls=%async_computation.14 | async-start | bytes 3538944
  412.6 39.0 %copy-start.24 = (f32[256,768]{1,0:T(8,128)}, f32[256,768]{1,0:T(8,128)S(1)}, u32[]{:S(2)}) copy-start(f32[256,768]{1,0:T(8,128)S(1)} %get-tuple-element.1037) | copy-start | bytes 2359300
  451.6 7.0 copy-start.31
  453.6 11.7 copy-start.22
  453.7 11.7 copy-start.55
  554.0 416.8 %reduce-scatter.13.cloned.1.call-start = ((), (), s32[]{:S(2)}) async-start(), calls=%async_computation.11 | async-start | bytes 7077888 | tf_op jit(solution)/shard_map/reduce_scatter | solution.py:291
  567.8 6.4 copy-start.5
  602.8 6.4 copy-start.5
  637.7 6.4 copy-start.5
  672.5 6.4 copy-start.5
  707.4 6.4 copy-start.5
  854.1 166.3 %reduce-scatter.21.cloned.1.call-start = ((), (), s32[]{:S(2)}) async-start(), calls=%async_computation.15 | async-start | bytes 5898240
  869.5 232.2 %reduce-scatter.17.cloned.1.call-start = ((), (), s32[]{:S(2)}) async-start(), calls=%async_computation.13 | async-start | bytes 11796480 | tf_op jit(solution)/shard_map/reduce_scatter | solution.py:209
  879.4 91.5 %copy-start.30 = (bf16[1,256,768]{2,1,0:T(8,128)(2,1)S(1)}, bf16[1,256,768]{2,1,0:T(8,128)(2,1)}, u32[]{:S(2)}) copy-start(bf16[1,256,768]{2,1,0:T(8,128)(2,1)} %param.18) | copy-start | bytes 1179652
  879.4 91.5 %copy-start.49 = (f32[768]{0:T(1024)S(1)}, f32[768]{0:T(1024)}, u32[]{:S(2)}) copy-start(f32[768]{0:T(1024)} %copy-done.48) | copy-start | bytes 9220
  879.4 91.5 %copy-start.54 = (f32[256]{0:T(256)S(1)}, f32[256]{0:T(256)}, u32[]{:S(2)}) copy-start(f32[256]{0:T(256)} %copy-done.53) | copy-start | bytes 3076
  879.4 273.3 %reduce-scatter.15.cloned.1.call-start = ((), (), s32[]{:S(2)}) async-start(), calls=%async_computation.12 | async-start | bytes 5898240 | tf_op jit(solution)/shard_map/reduce_scatter | solution.py:300
  976.3 199.7 %reduce-scatter.23.cloned.1.call-start = ((), (), s32[]{:S(2)}) async-start(), calls=%async_computation.16 | async-start | bytes 491520
  983.1 378.2 %all-reduce.9.cloned.1.call-start = ((), (), s32[]{:S(2)}) async-start(), calls=%async_computation.17 | async-start | bytes 10223616 | tf_op jit(solution)/shard_map/psum | solution.py:316
  1022.9 129.8 %copy-start.64 = (u32[32]{0:T(128)S(1)}, u32[32]{0:T(128)}, u32[]{:S(2)}) copy-start(u32[32]{0:T(128)} %constant.353) | copy-start | bytes 388
  (143 other events, 301.9 us)
Sparse Core Ops, SparseCore 0:
  9.6 40.1 all-gather.10
  51.3 37.4 all-gather.6
  91.6 60.4 all-gather.12
  154.7 97.6 all-gather.8
  253.8 62.4 all-gather.14
  554.1 72.5 reduce-scatter.18
  854.2 116.5 reduce-scatter.12
  973.4 46.9 reduce-scatter.20
  1023.2 78.4 reduce-scatter.16
  1104.8 47.8 reduce-scatter.14
  1155.1 20.8 reduce-scatter.22
  1180.4 180.8 all-reduce.8
where the time goes:
time: 1390 us; the launch traced here: 1380 us
  waiting for transfers between devices  634 us (46%)
  matrix products  327 us (24%)
  local copies, waits for them, and re-layouts  255 us (18%)
  other arithmetic  99.5 us (7%)
  blocking collectives  42.3 us (3%)
  between operations  16 us (1%)
    psum x1, waiting for transfers between devices, body(): lax.psum(cross_grad, 'ctx').astype(jnp.float32)  161 us
    all_gather x1, waiting for transfers between devices, body(): lax.all_gather(key_values, 'ctx', axis=0, tiled=True)  88.4 us
    reduce_scatter x1, waiting for transfers between devices, body(): lax.psum_scatter(grad_key_full.astype(jnp.bfloat16), 'ctx', scatter_dimen...  88.1 us
    reduce_scatter x1, waiting for transfers between devices, body(): lax.psum_scatter(jnp.concatenate([upper, lower], axis=1).astype(jnp.bfloa...  78.7 us
    dot_general x43, matrix products, times_transposed(): lax.dot_general(left, right, (((1,), (1,)), ((), ())), preferred_element_...  69.3 us
    dot_general x16, matrix products, score_piece(): jnp.einsum('vei,vy->yei', bucket_match_counts, bias_table_rows, preferred...  56 us
    dot_general x16, local copies, waits for them, and re-layouts, score_piece(): jnp.einsum('vei,vy->yei', bucket_match_counts, bias_table_rows, preferred...  55.3 us
    all_gather x1, waiting for transfers between devices, body(): encoder_kv = lax.all_gather(encoder_local, 'ctx', axis=0, tiled=True)  51.9 us
  transfers between devices with their start and end apart: 12, of which 10 were waited for; matrix products, arithmetic and copies ran while one was open for 38% of the time, Pallas kernels for 0%

commit v1 on v0

v1 whole, which is shorter than its diff:
```python
import functools

import jax
import jax.numpy as jnp
from jax import lax
from jax.experimental import pallas as pl
from jax.experimental.pallas import tpu as pltpu
from jax.sharding import PartitionSpec as P

NEGATIVE = -1e30
LANES = 128
VMEM_BYTES = 56 * 2**20


def dot(left, right):
    return lax.dot_general(
        left, right, (((1,), (0,)), ((), ())), preferred_element_type=jnp.float32
    )


def dot_t(left, right):
    return lax.dot_general(
        left, right, (((1,), (1,)), ((), ())), preferred_element_type=jnp.float32
    )


def t_dot(left, right):
    return lax.dot_general(
        left, right, (((0,), (0,)), ((), ())), preferred_element_type=jnp.float32
    )


def head_lanes(shape, head, head_size):
    lane = lax.broadcasted_iota(jnp.int32, shape, len(shape) - 1)
    return (lane >= head * head_size) & (lane < (head + 1) * head_size)


def only_head(values, head, head_size):
    return jnp.where(head_lanes(values.shape, head, head_size), values, jnp.zeros_like(values))


def tile_kernel(vector_ref, tile_ref):
    size = tile_ref.shape[-1]
    for head in range(vector_ref.shape[0]):
        for step in range(vector_ref.shape[1]):
            row = jnp.broadcast_to(
                vector_ref[head, step : step + 1, :], (size, 2 * size)
            )
            rolled = pltpu.roll(row, 0, 1, stride=1, stride_axis=0)
            tile_ref[head, step] = rolled[:, :size].astype(jnp.bfloat16)


def bias_tiles(vectors, group):
    head_count, steps, width = vectors.shape
    size = width // 2
    return pl.pallas_call(
        tile_kernel,
        grid=(head_count // group,),
        in_specs=[pl.BlockSpec((group, steps, width), lambda g: (g, 0, 0))],
        out_specs=pl.BlockSpec((group, steps, size, size), lambda g: (g, 0, 0, 0)),
        out_shape=jax.ShapeDtypeStruct((head_count, steps, size, size), jnp.bfloat16),
        compiler_params=pltpu.CompilerParams(vmem_limit_bytes=VMEM_BYTES),
        name="bias_tiles",
    )(vectors)


def forward_kernel(head_size, biased, *refs):
    if biased:
        place_ref, q_ref, k_ref, v_ref, tile_ref, out_ref, weight_ref, inverse_ref, score_ref = refs
    else:
        q_ref, k_ref, v_ref, out_ref, weight_ref, inverse_ref, score_ref = refs
    rows, key_total = q_ref.shape[0], k_ref.shape[0]
    group = q_ref.shape[1] // head_size
    piece = LANES
    out = jnp.zeros(q_ref.shape, jnp.float32)
    for head in range(group):
        query = only_head(q_ref[...], head, head_size)
        tops = [None] * (rows // piece)
        wide = 512
        for start in range(0, key_total, wide):
            scores = dot_t(query, k_ref[start : start + wide, :])
            for half in range(rows // piece):
                for part in range(wide // piece):
                    block = scores[
                        half * piece : (half + 1) * piece, part * piece : (part + 1) * piece
                    ]
                    key_block = start // piece + part
                    if biased:
                        place = place_ref[half * (key_total // piece) + key_block]
                        block = block + tile_ref[head, place].astype(jnp.float32)
                    score_ref[
                        half * piece : (half + 1) * piece,
                        key_block * piece : (key_block + 1) * piece,
                    ] = block
                    tops[half] = block if tops[half] is None else jnp.maximum(tops[half], block)
        top = jnp.concatenate([jnp.max(t, axis=1, keepdims=True) for t in tops], axis=0)
        total = jnp.zeros((rows, piece), jnp.float32)
        for start in range(0, key_total, piece):
            weights = jnp.exp(score_ref[:, start : start + piece] - top)
            total = total + weights
            weight_ref[head, :, start : start + piece] = weights.astype(jnp.bfloat16)
        inverse = 1.0 / jnp.sum(total, axis=1, keepdims=True)
        inverse_ref[head] = jnp.broadcast_to(inverse, (rows, LANES))
        mixed = dot(weight_ref[head], v_ref[...]) * inverse
        out = jnp.where(head_lanes(out.shape, head, head_size), mixed, out)
    out_ref[...] = out.astype(jnp.bfloat16)


def attention_forward(queries, key_values, head_size, tiles=None, places=None):
    rows, width = queries.shape
    key_total = key_values.shape[0]
    pairs = width // LANES
    group = LANES // head_size
    column = lambda shift: (lambda g, *_: (0, g + shift))
    in_specs = [
        pl.BlockSpec((rows, LANES), column(0)),
        pl.BlockSpec((key_total, LANES), column(0)),
        pl.BlockSpec((key_total, LANES), column(pairs)),
    ]
    operands = [queries, key_values, key_values]
    if tiles is not None:
        in_specs.append(
            pl.BlockSpec((group,) + tiles.shape[1:], lambda g, *_: (g, 0, 0, 0))
        )
        operands.append(tiles)
    grid_spec = pltpu.PrefetchScalarGridSpec(
        num_scalar_prefetch=0 if tiles is None else 1,
        grid=(pairs,),
        in_specs=in_specs,
        out_specs=[
            pl.BlockSpec((rows, LANES), column(0)),
            pl.BlockSpec((group, rows, key_total), lambda g, *_: (g, 0, 0)),
            pl.BlockSpec((group, rows, LANES), lambda g, *_: (g, 0, 0)),
        ],
        scratch_shapes=[pltpu.VMEM((rows, key_total), jnp.float32)],
    )
    heads = width // head_size
    return pl.pallas_call(
        functools.partial(forward_kernel, head_size, tiles is not None),
        grid_spec=grid_spec,
        out_shape=[
            jax.ShapeDtypeStruct((rows, width), jnp.bfloat16),
            jax.ShapeDtypeStruct((heads, rows, key_total), jnp.bfloat16),
            jax.ShapeDtypeStruct((heads, rows, LANES), jnp.float32),
        ],
        compiler_params=pltpu.CompilerParams(vmem_limit_bytes=VMEM_BYTES),
        cost_estimate=pl.CostEstimate(
            flops=8 * rows * key_total * width,
            bytes_accessed=2 * heads * rows * key_total + 4 * key_total * width,
            transcendentals=heads * rows * key_total,
        ),
        name="attention_forward",
    )(*(() if places is None else (places,)), *operands)


def backward_kernel(head_size, biased, *refs):
    if biased:
        (place_ref, q_ref, k_ref, v_ref, grad_ref, out_ref, weight_ref, inverse_ref,
         dq_ref, dkv_ref, dist_ref, ds_ref, sum_ref) = refs
    else:
        (q_ref, k_ref, v_ref, grad_ref, out_ref, weight_ref, inverse_ref,
         dq_ref, dkv_ref, ds_ref) = refs
    rows, key_total = q_ref.shape[0], k_ref.shape[0]
    group = q_ref.shape[1] // head_size
    piece = LANES
    wide = 512
    dq = jnp.zeros(q_ref.shape, jnp.float32)
    grads = grad_ref[...].astype(jnp.float32)
    deltas = grads * out_ref[...].astype(jnp.float32)
    if biased:
        sum_ref[...] = jnp.zeros_like(sum_ref)
    scaled_all = []
    for head in range(group):
        inverse = inverse_ref[head]
        scaled = only_head((grads * inverse).astype(jnp.bfloat16), head, head_size)
        scaled_all.append(scaled)
        delta = jnp.sum(only_head(deltas, head, head_size), axis=1, keepdims=True) * inverse
        for start in range(0, key_total, wide):
            grad_probs = dot_t(scaled, v_ref[start : start + wide, :])
            for half in range(rows // piece):
                for part in range(wide // piece):
                    lo = half * piece
                    at = start + part * piece
                    block = grad_probs[lo : lo + piece, part * piece : (part + 1) * piece]
                    weights = weight_ref[head, lo : lo + piece, at : at + piece]
                    change = weights.astype(jnp.float32) * (block - delta[lo : lo + piece])
                    ds_ref[head * rows + lo : head * rows + lo + piece, at : at + piece] = (
                        change.astype(jnp.bfloat16)
                    )
                    if biased:
                        place = place_ref[half * (key_total // piece) + at // piece]
                        sum_ref[head, place] += change
        mixed = dot(ds_ref[head * rows : (head + 1) * rows, :], k_ref[...])
        dq = jnp.where(head_lanes(dq.shape, head, head_size), mixed, dq)
    dq_ref[...] = dq.astype(jnp.bfloat16)
    queries = jnp.concatenate(
        [only_head(q_ref[...], head, head_size) for head in range(group)], axis=0
    )
    scaled_rows = jnp.concatenate(scaled_all, axis=0)
    for start in range(0, key_total, wide):
        dkv_ref[0, start : start + wide, :] = t_dot(
            ds_ref[:, start : start + wide], queries
        ).astype(jnp.bfloat16)
        weights = jnp.concatenate(
            [weight_ref[head, :, start : start + wide] for head in range(group)], axis=0
        )
        dkv_ref[1, start : start + wide, :] = t_dot(weights, scaled_rows).astype(
            jnp.bfloat16
        )
    if biased:
        steps = dist_ref.shape[1]
        down = lax.broadcasted_iota(jnp.int32, (piece, piece), 0)
        across = lax.broadcasted_iota(jnp.int32, (piece, piece), 1)
        flip = (down + across == piece - 1).astype(jnp.bfloat16)

        def fold(step, carry):
            for head in range(group):
                block = sum_ref[head, step]
                high = block.astype(jnp.bfloat16)
                low = (block - high.astype(jnp.float32)).astype(jnp.bfloat16)
                turned = dot(flip, high) + dot(flip, low)
                padded = jnp.concatenate([turned, jnp.zeros_like(turned)], axis=1)
                rolled = pltpu.roll(padded, piece + 1, 1, stride=1, stride_axis=0)
                dist_ref[head, pl.ds(step, 1), :] = jnp.sum(rolled, axis=0, keepdims=True)
            return carry

        lax.fori_loop(0, steps, fold, 0)


def attention_backward(
    queries, key_values, grads, outs, weights, inverses, head_size, places=None, steps=0
):
    rows, width = queries.shape
    key_total = key_values.shape[0]
    pairs = width // LANES
    group = LANES // head_size
    heads = width // head_size
    biased = places is not None
    column = lambda shift: (lambda g, *_: (0, g + shift))
    row_block = pl.BlockSpec((rows, LANES), column(0))
    key_block = pl.BlockSpec((key_total, LANES), column(0))
    out_specs = [row_block, pl.BlockSpec((2, key_total, LANES), lambda g, *_: (0, 0, g))]
    out_shape = [
        jax.ShapeDtypeStruct((rows, width), jnp.bfloat16),
        jax.ShapeDtypeStruct((2, key_total, width), jnp.bfloat16),
    ]
    scratch = [pltpu.VMEM((group * rows, key_total), jnp.bfloat16)]
    if biased:
        out_specs.append(pl.BlockSpec((group, steps, 2 * LANES), lambda g, *_: (g, 0, 0)))
        out_shape.append(jax.ShapeDtypeStruct((heads, steps, 2 * LANES), jnp.float32))
        scratch.append(pltpu.VMEM((group, steps + 1, LANES, LANES), jnp.float32))
    grid_spec = pltpu.PrefetchScalarGridSpec(
        num_scalar_prefetch=1 if biased else 0,
        grid=(pairs,),
        in_specs=[
            row_block,
            key_block,
            pl.BlockSpec((key_total, LANES), column(pairs)),
            row_block,
            row_block,
            pl.BlockSpec((group, rows, key_total), lambda g, *_: (g, 0, 0)),
            pl.BlockSpec((group, rows, LANES), lambda g, *_: (g, 0, 0)),
        ],
        out_specs=out_specs,
        scratch_shapes=scratch,
    )
    return pl.pallas_call(
        functools.partial(backward_kernel, head_size, biased),
        grid_spec=grid_spec,
        out_shape=out_shape,
        compiler_params=pltpu.CompilerParams(vmem_limit_bytes=VMEM_BYTES),
        cost_estimate=pl.CostEstimate(
            flops=16 * rows * key_total * width,
            bytes_accessed=2 * heads * rows * key_total + 8 * key_total * width,
            transcendentals=0,
        ),
        name="attention_backward",
    )(
        *((places,) if biased else ()),
        queries, key_values, key_values, grads, outs, weights, inverses,
    )


EPSILON = 1e-06


def row_norm(values, gain):
    return values * lax.rsqrt(jnp.mean(values * values, axis=-1, keepdims=True) + EPSILON) * gain


def gated_gelu(gate_up):
    hidden_units = gate_up.shape[1] // 2
    return jax.nn.gelu(gate_up[:, :hidden_units], approximate=True) * gate_up[:, hidden_units:]


def rounded(values):
    return values.astype(jnp.bfloat16)


def distance_rows(by_distance, block):
    heads = by_distance.shape[0]
    padded = jnp.concatenate(
        [
            jnp.full((heads, block - 1), NEGATIVE, jnp.float32),
            by_distance,
            jnp.full((heads, 1), NEGATIVE, jnp.float32),
        ],
        axis=1,
    )
    pieces = padded.reshape(heads, -1, block)[:, :, ::-1]
    rows = jnp.concatenate([pieces[:, :-1], pieces[:, 1:]], axis=2)
    return jnp.concatenate([rows, jnp.full((heads, 1, 2 * block), NEGATIVE, jnp.float32)], axis=1)


def by_distance_sums(rows, block):
    heads, steps, _ = rows.shape
    zero = jnp.zeros((heads, 1, block), jnp.float32)
    pieces = jnp.concatenate([rows[:, :, :block], zero], axis=1) + jnp.concatenate(
        [zero, rows[:, :, block:]], axis=1
    )
    return pieces[:, :, ::-1].reshape(heads, -1)[:, block - 1 : block - 1 + steps * block]


def reduce_weight(grad):
    share = lax.psum_scatter(rounded(grad), ("fsdp", "ctx"), scatter_dimension=0, tiled=True)
    return lax.all_gather(share, "ctx", axis=0, tiled=True).astype(jnp.float32)


def body(tokens, encoded, cotangent, w_self, w_cross, w_ffn, gains, table, bucket_ids, block_order):
    row_count = tokens.shape[1]
    model_width = tokens.shape[2]
    head_count = table.shape[1]
    head_size = model_width // head_count
    hidden_units = w_ffn.shape[1] // 3
    block = row_count // 2
    seq_length = bucket_ids.shape[0]
    steps = seq_length // block
    ctx_place = lax.axis_index("ctx")
    table_rows = lax.all_gather(table, "fsdp", axis=0, tiled=True)
    gain_rows = lax.all_gather(gains, "fsdp", axis=1, tiled=True)
    whole_self = lax.all_gather(w_self, "fsdp", axis=0, tiled=True)
    whole_cross = lax.all_gather(w_cross, "fsdp", axis=0, tiled=True)
    whole_ffn = lax.all_gather(w_ffn, "fsdp", axis=0, tiled=True)
    gain_float = gain_rows.astype(jnp.float32)
    bucket_count = table_rows.shape[0]
    in_bucket = (
        bucket_ids[None, :] == jnp.arange(bucket_count, dtype=jnp.int32)[:, None]
    ).astype(jnp.float32)
    by_distance = lax.dot_general(
        table_rows.astype(jnp.float32),
        in_bucket,
        (((0,), (0,)), ((), ())),
        precision=lax.Precision.HIGHEST,
    )
    tiles = bias_tiles(distance_rows(by_distance, block), LANES // head_size)
    own_blocks = lax.dynamic_slice_in_dim(block_order, 2 * ctx_place, 2)
    apart = own_blocks[:, None] - block_order[None, :]
    places = jnp.where(apart < 0, steps, apart).astype(jnp.int32).reshape(-1)

    inputs = tokens[0].astype(jnp.float32)
    encoder_rows = encoded[0]
    normed_one = rounded(row_norm(inputs, gain_float[0]))
    projected = rounded(dot(normed_one, whole_self[:, : 3 * model_width]))
    queries = projected[:, :model_width]
    key_values = lax.all_gather(projected[:, model_width:], "ctx", axis=0, tiled=True)
    encoder_local = rounded(dot(encoder_rows, whole_cross[:, model_width : 3 * model_width]))
    encoder_kv = lax.all_gather(encoder_local, "ctx", axis=0, tiled=True)
    attended, weights, inverses = attention_forward(queries, key_values, head_size, tiles, places)
    after_one = inputs + dot(attended, whole_self[:, 3 * model_width :])
    normed_two = rounded(row_norm(after_one, gain_float[1]))
    cross_query = rounded(dot(normed_two, whole_cross[:, :model_width]))
    cross_rows, cross_weights, cross_inverses = attention_forward(
        cross_query, encoder_kv, head_size
    )
    after_two = after_one + dot(cross_rows, whole_cross[:, 3 * model_width :])
    normed_three = rounded(row_norm(after_two, gain_float[2]))
    gate_up = dot(normed_three, whole_ffn[:, : 2 * hidden_units])
    mixed_float, gated_back = jax.vjp(gated_gelu, gate_up)
    mixed_rows = rounded(mixed_float)
    output = rounded(after_two + dot_t(mixed_rows, whole_ffn[:, 2 * hidden_units :]))

    grad_branch_three = cotangent[0]
    grad_after_two = grad_branch_three.astype(jnp.float32)
    grad_mixed = dot(grad_branch_three, whole_ffn[:, 2 * hidden_units :])
    grad_gate_up = rounded(gated_back(grad_mixed)[0])
    grad_normed_three = dot_t(grad_gate_up, whole_ffn[:, : 2 * hidden_units])
    ffn_grad = reduce_weight(
        jnp.concatenate(
            [
                rounded(t_dot(normed_three, grad_gate_up)),
                rounded(t_dot(grad_branch_three, mixed_rows)),
            ],
            axis=1,
        )
    )
    norm_part, gain_three = jax.vjp(row_norm, after_two, gain_float[2])[1](grad_normed_three)
    grad_after_one = grad_after_two + norm_part
    grad_branch_two = rounded(grad_after_one)
    grad_cross_rows = rounded(dot_t(grad_branch_two, whole_cross[:, 3 * model_width :]))
    grad_cross_query, encoder_full = attention_backward(
        cross_query, encoder_kv, grad_cross_rows, cross_rows, cross_weights, cross_inverses,
        head_size,
    )
    encoder_own = lax.psum_scatter(encoder_full, "ctx", scatter_dimension=1, tiled=True)
    grad_normed_two = dot_t(grad_cross_query, whole_cross[:, :model_width])
    norm_part, gain_two = jax.vjp(row_norm, after_one, gain_float[1])[1](grad_normed_two)
    grad_inputs_one = grad_after_one + norm_part
    grad_branch_one = rounded(grad_inputs_one)
    grad_attended = rounded(dot_t(grad_branch_one, whole_self[:, 3 * model_width :]))
    grad_query, grad_key_full, distance_sums = attention_backward(
        queries, key_values, grad_attended, attended, weights, inverses, head_size, places, steps
    )
    grad_key_own = lax.psum_scatter(grad_key_full, "ctx", scatter_dimension=1, tiled=True)

    grad_encoder_kv = jnp.concatenate([encoder_own[0], encoder_own[1]], axis=1)
    grad_encoded = rounded(
        dot_t(grad_encoder_kv, whole_cross[:, model_width : 3 * model_width])
    )
    cross_grad = reduce_weight(
        jnp.concatenate(
            [
                rounded(t_dot(normed_two, grad_cross_query)),
                rounded(t_dot(encoder_rows, grad_encoder_kv)),
                rounded(t_dot(cross_rows, grad_branch_two)),
            ],
            axis=1,
        )
    )
    grad_table = lax.dot_general(
        in_bucket,
        by_distance_sums(distance_sums, block),
        (((1,), (1,)), ((), ())),
        precision=lax.Precision.HIGHEST,
    )
    grad_projected = jnp.concatenate([grad_query, grad_key_own[0], grad_key_own[1]], axis=1)
    grad_normed_one = dot_t(grad_projected, whole_self[:, : 3 * model_width])
    self_grad = reduce_weight(
        jnp.concatenate(
            [
                rounded(t_dot(normed_one, grad_projected)),
                rounded(t_dot(attended, grad_branch_one)),
            ],
            axis=1,
        )
    )
    norm_part, gain_one = jax.vjp(row_norm, inputs, gain_float[0])[1](grad_normed_one)
    grad_tokens = rounded(grad_inputs_one + norm_part)
    gain_terms = jnp.stack([gain_one, gain_two, gain_three])
    small = jnp.concatenate([gain_terms.reshape(-1), grad_table.reshape(-1)])
    small = lax.psum(small, ("fsdp", "ctx"))
    fsdp_place = lax.axis_index("fsdp")
    gain_total = small[: gain_terms.size].reshape(gain_terms.shape)
    table_total = small[gain_terms.size :].reshape(grad_table.shape)
    gain_own = lax.dynamic_slice_in_dim(
        gain_total, fsdp_place * gains.shape[1], gains.shape[1], axis=1
    )
    table_own = lax.dynamic_slice_in_dim(
        table_total, fsdp_place * table.shape[0], table.shape[0], axis=0
    )
    return (
        output[None],
        grad_tokens[None],
        grad_encoded[None],
        self_grad,
        cross_grad,
        ffn_grad,
        gain_own,
        table_own,
    )


def solution(mesh):
    in_specs = (
        P("fsdp", "ctx", None),
        P("fsdp", "ctx", None),
        P("fsdp", "ctx", None),
        P("fsdp", None),
        P("fsdp", None),
        P("fsdp", None),
        P(None, "fsdp"),
        P("fsdp", None),
        P(),
        P(),
    )
    out_specs = (
        P("fsdp", "ctx", None),
        P("fsdp", "ctx", None),
        P("fsdp", "ctx", None),
        P("fsdp", None),
        P("fsdp", None),
        P("fsdp", None),
        P(None, "fsdp"),
        P("fsdp", None),
    )
    return jax.shard_map(body, mesh=mesh, in_specs=in_specs, out_specs=out_specs, check_vma=False)
```

time: 1390 us -> 1050 us (0.76)
  matrix products: 327 us -> 55.6 us
  local copies, waits for them, and re-layouts: 255 us -> 18.6 us
  waiting for transfers between devices: 634 us -> 789 us
  Pallas kernels: 0 us -> 96.4 us
  other arithmetic: 99.5 us -> 22.8 us
    dot_general x185 -> x23, matrix products: 327 us -> 55.6 us  [the longest x7 21 us: dot(): lax.dot_general(left, right, (((1,), (0,)), ((), ())), preferred_element_...]
    reduce_scatter x3 -> x5, waiting for transfers between devices: 218 us -> 468 us  [the longest x3 355 us: reduce_weight(): lax.psum_scatter(rounded(grad), ('fsdp', 'ctx'), scatter_dimension=0, til...]
    psum x1 -> x0, waiting for transfers between devices: 161 us -> none  [body(): lax.psum(cross_grad, 'ctx').astype(jnp.float32)]
    pallas_call x0 -> x5, Pallas kernels: none -> 96.4 us  [the longest x2 60.5 us: attention_backward(): pl.pallas_call(functools.partial(backward_kernel, head_size, biased), gri...]
    slice x39 -> x8, local copies, waits for them, and re-layouts: 82.2 us -> 1.94 us  [the longest x1 0.93 us: body(): projected[:, model_width:]]
    all_gather x2 -> x5, waiting for transfers between devices: 119 us -> 195 us  [the longest x1 83.5 us: body(): lax.all_gather(projected[:, model_width:], 'ctx', axis=0, tiled=True)]
    dot_general x16 -> x0, local copies, waits for them, and re-layouts: 55.3 us -> none  [score_piece(): jnp.einsum('vei,vy->yei', bucket_match_counts, bias_table_rows, preferred...]
    all_gather x1, waiting for transfers between devices: 0.02 us -> 51.2 us  [body(): whole_ffn = lax.all_gather(w_ffn, 'fsdp', axis=0, tiled=True)]
  transfers between devices with their start and end apart: 12 -> 13, of which waited for: 10 -> 12; matrix products, arithmetic and copies ran while one was open for 38% -> 7% of each run, Pallas kernels for 0% -> 8%
where the time goes in v1:
time: 1050 us
  waiting for transfers between devices  789 us (75%)
  Pallas kernels  96.4 us (9%)
  matrix products  55.6 us (5%)
  blocking collectives  51.8 us (5%)
  other arithmetic  22.8 us (2%)
  local copies, waits for them, and re-layouts  18.6 us (2%)
  between operations  14.5 us (1%)
    reduce_scatter x3, waiting for transfers between devices, reduce_weight(): lax.psum_scatter(rounded(grad), ('fsdp', 'ctx'), scatter_dimension=0, til...  355 us
    reduce_scatter x1, waiting for transfers between devices, body(): lax.psum_scatter(grad_key_full, 'ctx', scatter_dimension=1, tiled=True)  97.2 us
    all_gather x1, waiting for transfers between devices, body(): lax.all_gather(projected[:, model_width:], 'ctx', axis=0, tiled=True)  83.5 us
    all_gather x3, waiting for transfers between devices, reduce_weight(): return lax.all_gather(share, 'ctx', axis=0, tiled=True).astype(jnp.float32)  77 us
    pallas_call x2, Pallas kernels, attention_backward(): pl.pallas_call(functools.partial(backward_kernel, head_size, biased), gri...  60.5 us
    all_gather x1, waiting for transfers between devices, body(): whole_ffn = lax.all_gather(w_ffn, 'fsdp', axis=0, tiled=True)  51.2 us
    psum x1, blocking collectives, body(): small = lax.psum(small, ('fsdp', 'ctx'))  40.6 us
    all_gather x1, waiting for transfers between devices, body(): encoder_kv = lax.all_gather(encoder_local, 'ctx', axis=0, tiled=True)  38.1 us
  transfers between devices with their start and end apart: 13, of which 12 were waited for; matrix products, arithmetic and copies ran while one was open for 7% of the time, Pallas kernels for 8%

profile of v1, /device:TPU:0, one launch (start us, length us, event | category | flops | bytes accessed | tf_op | source)
XLA Modules:
  0.0 1049.8 jit_solution(31827003041379514)
XLA Ops:
  8.7 6.1 all-gather
  15.2 34.6 %all-gather.10.cloned.1.call-done = bf16[768,3072]{1,0:T(8,128)(2,1)} async-done(((bf16[192,3072]{1,0:T(8,128)(2,1)}), bf16[768,3072]{1,0:T(8,128)(2,1)}) %all-gather.10.cloned.1.call-update) | async-done | bytes 4718608 | tf_op jit(solution)/shard_map/all_gather | solution.py:341
  49.8 3.1 convolution_convert_fusion.2
  54.0 34.9 %all-gather.14.cloned.1.call-done = bf16[768,3072]{1,0:T(8,128)(2,1)} async-done(((bf16[192,3072]{1,0:T(8,128)(2,1)}), bf16[768,3072]{1,0:T(8,128)(2,1)}) %all-gather.14.cloned.1.call-update) | async-done | bytes 4718608 | tf_op jit(solution)/shard_map/all_gather | solution.py:342
  88.8 2.9 convolution_convert_fusion.5
  92.6 5.2 all_gather.33
  99.1 6.7 bias_tiles.1.refs_4_
  107.2 83.5 %all-gather.12.cloned.1.call-done.refs_2_.refs_3_ = bf16[2048,1536]{1,0:T(8,128)(2,1)} async-done(((bf16[256,1536]{1,0:T(8,128)(2,1)}), bf16[2048,1536]{1,0:T(8,128)(2,1)}) %all-gather.12.cloned.1.call-update) | async-done | bytes 6291472 | tf_op jit(solution)/shard_map/all_gather | solution.py:365
  190.7 18.6 %attention_forward.2 = (bf16[256,768]{1,0:T(8,128)(2,1)}, bf16[12,256,2048]{2,1,0:T(8,128)(2,1)}, f32[12,256,128]{2,1,0:T(8,128)}) custom-call(s32[32]{0:T(128)} %compare_select_fusion.refs_0_, bf16[256,768]{1,0:T(8,128)(2,1)} %slice.128.refs_1_, bf16[2048,1536]{1,0:T(8,128)(2,1)} %all-gather.12.cloned.1.call-done.refs_2_.refs_3_, ...), custom_call_target="tpu_custom_call" | custom-call | flops 3221225472 | bytes 18874368 | tf_op jit(solution)/shard_map/attention_forward/pallas_call | solution.py:138
  213.8 38.1 %all-gather.16.cloned.1.call-done.refs_1_.refs_2_ = bf16[1024,1536]{1,0:T(8,128)(2,1)} async-done(((bf16[128,1536]{1,0:T(8,128)(2,1)}), bf16[1024,1536]{1,0:T(8,128)(2,1)}) %all-gather.16.cloned.1.call-update) | async-done | bytes 3145744 | tf_op jit(solution)/shard_map/all_gather | solution.py:367
  251.9 10.6 %attention_forward.3 = (bf16[256,768]{1,0:T(8,128)(2,1)}, bf16[12,256,1024]{2,1,0:T(8,128)(2,1)}, f32[12,256,128]{2,1,0:T(8,128)}) custom-call(bf16[256,768]{1,0:T(8,128)(2,1)} %convolution_convert_fusion.11.refs_0_, bf16[1024,1536]{1,0:T(8,128)(2,1)} %all-gather.16.cloned.1.call-done.refs_1_.refs_2_, ...), custom_call_target="tpu_custom_call" | custom-call | flops 1610612736 | bytes 9437184 | tf_op jit(solution)/shard_map/attention_forward/pallas_call | solution.py:138
  265.0 51.2 %all-gather.18.cloned.1.call-done = bf16[768,6144]{1,0:T(8,128)(2,1)} async-done(((bf16[192,6144]{1,0:T(8,128)(2,1)}), bf16[768,6144]{1,0:T(8,128)(2,1)}) %all-gather.18.cloned.1.call-update) | async-done | bytes 9437200 | tf_op jit(solution)/shard_map/all_gather | solution.py:343
  316.2 4.8 fusion.2
  321.8 3.3 fusion.54
  330.5 11.5 %attention_backward.2 = (bf16[256,768]{1,0:T(8,128)(2,1)}, bf16[2,1024,768]{2,1,0:T(8,128)(2,1)}) custom-call(bf16[256,768]{1,0:T(8,128)(2,1)} %convolution_convert_fusion.11.refs_0_, bf16[1024,1536]{1,0:T(8,128)(2,1)} %all-gather.16.cloned.1.call-done.refs_1_.refs_2_, bf16[1024,1536]{1,0:T(8,128)(2,1)} %all-gather.16.cloned.1.call-done.refs_1_.refs_2_, ...), custom_call_target="tpu_custom_call" | custom-call | flops 3221225472 | bytes 12582912 | tf_op jit(solution)/shard_map/attention_backward/pallas_call | solution.py:267
  348.2 49.0 %attention_backward.3 = (bf16[256,768]{1,0:T(8,128)(2,1)}, bf16[2,2048,768]{2,1,0:T(8,128)(2,1)}, f32[12,16,256]{2,1,0:T(8,128)}) custom-call(s32[32]{0:T(128)} %compare_select_fusion.refs_0_, bf16[256,768]{1,0:T(8,128)(2,1)} %slice.128.refs_1_, bf16[2048,1536]{1,0:T(8,128)(2,1)} %all-gather.12.cloned.1.call-done.refs_2_.refs_3_, ...), custom_call_target="tpu_custom_call" | custom-call | flops 6442450944 | bytes 25165824 | tf_op jit(solution)/shard_map/attention_backward/pallas_call | solution.py:267
  401.5 15.2 %reduce-scatter.10.cloned.1.call-done = bf16[2,128,768]{2,1,0:T(8,128)(2,1)} async-done(((bf16[2,1024,768]{2,1,0:T(8,128)(2,1)}), bf16[2,128,768]{2,1,0:T(8,128)(2,1)}) %reduce-scatter.10.cloned.1.call-update) | async-done | bytes 393232 | tf_op jit(solution)/shard_map/reduce_scatter | solution.py:404
  421.2 6.8 copy.39
  433.4 4.1 pad_maximum_fusion
  440.2 97.2 %reduce-scatter.8.cloned.1.call-done = bf16[2,256,768]{2,1,0:T(8,128)(2,1)} async-done(((bf16[2,2048,768]{2,1,0:T(8,128)(2,1)}), bf16[2,256,768]{2,1,0:T(8,128)(2,1)}) %reduce-scatter.8.cloned.1.call-update) | async-done | bytes 786448 | tf_op jit(solution)/shard_map/reduce_scatter | solution.py:413
  544.1 104.9 %reduce-scatter.16.cloned.1.call-done = bf16[24,3072]{1,0:T(8,128)(2,1)} async-done(((bf16[768,3072]{1,0:T(8,128)(2,1)}), bf16[24,3072]{1,0:T(8,128)(2,1)}) %reduce-scatter.16.cloned.1.call-update) | async-done | bytes 147472 | tf_op jit(solution)/shard_map/reduce_scatter | solution.py:325
  649.1 141.4 %reduce-scatter.14.cloned.1.call-done = bf16[24,6144]{1,0:T(8,128)(2,1)} async-done(((bf16[768,6144]{1,0:T(8,128)(2,1)}), bf16[24,6144]{1,0:T(8,128)(2,1)}) %reduce-scatter.14.cloned.1.call-update) | async-done | bytes 294928 | tf_op jit(solution)/shard_map/reduce_scatter | solution.py:325
  793.6 109.0 %reduce-scatter.12.cloned.1.call-done = bf16[24,3072]{1,0:T(8,128)(2,1)} async-done(((bf16[768,3072]{1,0:T(8,128)(2,1)}), bf16[24,3072]{1,0:T(8,128)(2,1)}) %reduce-scatter.12.cloned.1.call-update) | async-done | bytes 147472 | tf_op jit(solution)/shard_map/reduce_scatter | solution.py:325
  902.6 3.7 fusion.28
  906.3 3.3 fusion.34
  909.7 3.3 fusion.47
  913.0 40.6 %psum.7 = f32[2688]{0:T(1024)S(1)} all-reduce(f32[2688]{0:T(1024)S(1)} %pad_maximum_fusion.10), channel_id=1, replica_groups=mesh['ctx'=8,'fsdp'=4] {'fsdp','ctx'}, use_global_device_ids=true, to_apply=%region_14.15 | all-reduce | flops 2688 | bytes 21504 | tf_op jit(solution)/shard_map/psum | solution.py:450
  956.0 2.9 convert_element_type.121
  958.9 39.4 %all-gather.24.cloned.1.call-done = bf16[192,6144]{1,0:T(8,128)(2,1)} async-done(((bf16[24,6144]{1,0:T(8,128)(2,1)}), bf16[192,6144]{1,0:T(8,128)(2,1)}) %all-gather.24.cloned.1.call-update) | async-done | bytes 2359312 | tf_op jit(solution)/shard_map/all_gather | solution.py:326
  998.3 4.4 convert_element_type.125
  1002.7 37.6 %all-gather.20.cloned.1.call-done = bf16[192,3072]{1,0:T(8,128)(2,1)} async-done(((bf16[24,3072]{1,0:T(8,128)(2,1)}), bf16[192,3072]{1,0:T(8,128)(2,1)}) %all-gather.20.cloned.1.call-update) | async-done | bytes 1179664 | tf_op jit(solution)/shard_map/all_gather | solution.py:326
  1040.3 2.9 convert_element_type.116
  (161 shorter events, 54.5 us)
Async XLA Ops:
  7.2 81.7 %copy-start = (bf16[1,128,768]{2,1,0:T(8,128)(2,1)S(1)}, bf16[1,128,768]{2,1,0:T(8,128)(2,1)}, u32[]{:S(2)}) copy-start(bf16[1,128,768]{2,1,0:T(8,128)(2,1)} %param.11) | copy-start | bytes 589828
  7.2 7.8 copy-start.12
  7.2 42.6 %all-gather.10.cloned.1.call-start = ((), (), s32[]{:S(2)}) async-start(), calls=%async_computation.5 | async-start | bytes 5898240 | tf_op jit(solution)/shard_map/all_gather | solution.py:341
  7.9 80.9 %all-gather.14.cloned.1.call-start = ((), (), s32[]{:S(2)}) async-start(), calls=%async_computation.7 | async-start | bytes 5898240 | tf_op jit(solution)/shard_map/all_gather | solution.py:342
  8.7 182.0 %all-gather.12.cloned.1.call-start = ((), (), s32[]{:S(2)}) async-start(), calls=%async_computation.6 | async-start | bytes 7077888 | tf_op jit(solution)/shard_map/all_gather | solution.py:365
  15.0 523.6 %copy-start.24 = (f32[768]{0:T(1024)}, f32[768]{0:T(1024)S(1)}, u32[]{:S(2)}) copy-start(f32[768]{0:T(1024)S(1)} %get-tuple-element.54) | copy-start | bytes 9220
  15.2 37.8 %copy-start.26 = (f32[256]{0:T(256)}, f32[256]{0:T(256)S(1)}, u32[]{:S(2)}) copy-start(f32[256]{0:T(256)S(1)} %fusion.52) | copy-start | bytes 3076
  15.2 523.4 %copy-start.28 = (f32[256]{0:T(256)}, f32[256]{0:T(256)S(1)}, u32[]{:S(2)}) copy-start(f32[256]{0:T(256)S(1)} %fusion.70) | copy-start | bytes 3076
  53.9 38.5 %copy-start.32 = (s32[16]{0:T(128)S(1)}, s32[16]{0:T(128)}, u32[]{:S(2)}) copy-start(s32[16]{0:T(128)} %param.19) | copy-start | bytes 196
  53.9 38.7 %copy-start.31 = (bf16[8,12]{1,0:T(8,128)(2,1)S(1)}, bf16[8,12]{1,0:T(8,128)(2,1)}, u32[]{:S(2)}) copy-start(bf16[8,12]{1,0:T(8,128)(2,1)} %param.17) | copy-start | bytes 580
  53.9 43.9 %copy-start.23 = (s32[2048]{0:T(1024)S(1)}, s32[2048]{0:T(1024)}, u32[]{:S(2)}) copy-start(s32[2048]{0:T(1024)} %param.18) | copy-start | bytes 24580
  53.9 198.0 %all-gather.16.cloned.1.call-start = ((), (), s32[]{:S(2)}) async-start(), calls=%async_computation.8 | async-start | bytes 3538944 | tf_op jit(solution)/shard_map/all_gather | solution.py:367
  91.8 224.5 %all-gather.18.cloned.1.call-start = ((), (), s32[]{:S(2)}) async-start(), calls=%async_computation.9 | async-start | bytes 11796480 | tf_op jit(solution)/shard_map/all_gather | solution.py:343
  92.3 324.4 %reduce-scatter.10.cloned.1.call-start = ((), (), s32[]{:S(2)}) async-start(), calls=%async_computation.11 | async-start | bytes 3538944 | tf_op jit(solution)/shard_map/reduce_scatter | solution.py:404
  316.2 4.8 copy-start.10
  316.2 5.6 copy-start.33
  342.0 195.4 %reduce-scatter.8.cloned.1.call-start = ((), (), s32[]{:S(2)}) async-start(), calls=%async_computation.10 | async-start | bytes 7077888 | tf_op jit(solution)/shard_map/reduce_scatter | solution.py:413
  397.2 251.8 %reduce-scatter.16.cloned.1.call-start = ((), (), s32[]{:S(2)}) async-start(), calls=%async_computation.17 | async-start | bytes 4866048 | tf_op jit(solution)/shard_map/reduce_scatter | solution.py:325
  428.0 362.5 %reduce-scatter.14.cloned.1.call-start = ((), (), s32[]{:S(2)}) async-start(), calls=%async_computation.15 | async-start | bytes 9732096 | tf_op jit(solution)/shard_map/reduce_scatter | solution.py:325
  437.6 101.0 %copy-start.13 = (bf16[1,256,768]{2,1,0:T(8,128)(2,1)S(1)}, bf16[1,256,768]{2,1,0:T(8,128)(2,1)}, u32[]{:S(2)}) copy-start(bf16[1,256,768]{2,1,0:T(8,128)(2,1)} %param.10) | copy-start | bytes 1179652
  437.6 464.9 %reduce-scatter.12.cloned.1.call-start = ((), (), s32[]{:S(2)}) async-start(), calls=%async_computation.12 | async-start | bytes 4866048 | tf_op jit(solution)/shard_map/reduce_scatter | solution.py:325
  544.0 246.9 %copy-start.22 = (f32[12,16,256]{2,1,0:T(8,128)S(1)}, f32[12,16,256]{2,1,0:T(8,128)}, u32[]{:S(2)}) copy-start(f32[12,16,256]{2,1,0:T(8,128)} %get-tuple-element.29) | copy-start | bytes 589828
  544.0 411.9 %all-gather.22.cloned.1.call-start = ((), (), s32[]{:S(2)}) async-start(), calls=%async_computation.14 | async-start | bytes 1327104 | tf_op jit(solution)/shard_map/all_gather | solution.py:326
  649.0 349.3 %all-gather.24.cloned.1.call-start = ((), (), s32[]{:S(2)}) async-start(), calls=%async_computation.16 | async-start | bytes 2654208 | tf_op jit(solution)/shard_map/all_gather | solution.py:326
  790.5 249.8 %all-gather.20.cloned.1.call-start = ((), (), s32[]{:S(2)}) async-start(), calls=%async_computation.13 | async-start | bytes 1327104 | tf_op jit(solution)/shard_map/all_gather | solution.py:326
  902.6 3.7 copy-start.15
  906.3 3.3 copy-start.19
  906.3 3.3 copy-start.25
  906.3 3.3 copy-start.29
  906.3 3.3 copy-start.34
  909.6 45.3 %copy-start.27 = (f32[256]{0:T(256)S(1)}, f32[256]{0:T(256)}, u32[]{:S(2)}) copy-start(f32[256]{0:T(256)} %copy-done.26) | copy-start | bytes 3076
  998.3 45.0 %copy-start.1 = (bf16[1,128,768]{2,1,0:T(8,128)(2,1)S(1)}, bf16[1,128,768]{2,1,0:T(8,128)(2,1)}, u32[]{:S(2)}) copy-start(bf16[1,128,768]{2,1,0:T(8,128)(2,1)} %param.11) | copy-start | bytes 589828
  (16 other events, 35.0 us)
Sparse Core Ops, SparseCore 0:
  9.6 40.1 all-gather.9
  51.3 37.4 all-gather.13
  91.6 99.0 all-gather.11
  193.3 58.5 all-gather.15
  253.3 62.8 all-gather.17
  342.1 74.5 reduce-scatter.9
  420.3 117.0 reduce-scatter.7
  542.9 106.0 reduce-scatter.15
  655.9 134.5 reduce-scatter.13
  796.4 106.0 reduce-scatter.11
  905.0 40.3 all-gather.21
  947.6 50.6 all-gather.23
  1000.7 39.5 all-gather.19

commit v2 on v1

--- a/solution.py
+++ b/solution.py
@@ -1,4 +1,5 @@
 import functools
+import math
 
 import jax
 import jax.numpy as jnp
@@ -321,9 +322,95 @@
     return pieces[:, :, ::-1].reshape(heads, -1)[:, block - 1 : block - 1 + steps * block]
 
 
-def reduce_weight(grad):
-    share = lax.psum_scatter(rounded(grad), ("fsdp", "ctx"), scatter_dimension=0, tiled=True)
-    return lax.all_gather(share, "ctx", axis=0, tiled=True).astype(jnp.float32)
+def bit_count(axis_name):
+    return int(math.log2(lax.axis_size(axis_name)))
+
+
+def swap(values, axis_name, bit):
+    size = lax.axis_size(axis_name)
+    return lax.ppermute(values, axis_name, [(i, i ^ (1 << bit)) for i in range(size)])
+
+
+def own_bit(axis_name, bit):
+    return (lax.axis_index(axis_name) >> bit) & 1
+
+
+def pick(values, index, axis):
+    return lax.dynamic_index_in_dim(values, index, axis, keepdims=False)
+
+
+def gather_rows(share):
+    rows = share.shape[0]
+    place = lax.axis_index("fsdp")
+    whole = jnp.zeros((rows * lax.axis_size("fsdp"),) + share.shape[1:], share.dtype)
+    held = [(share, place)]
+    for bit in reversed(range(bit_count("fsdp"))):
+        held = held + [(swap(piece, "fsdp", bit), at ^ (1 << bit)) for piece, at in held]
+    for piece, at in held:
+        whole = lax.dynamic_update_slice_in_dim(whole, piece, at * rows, 0)
+    return whole
+
+
+class Product:
+    def __init__(self, left, right, parts):
+        bits = int(math.log2(parts))
+        self.left = left.reshape((left.shape[0],) + (2,) * bits + (left.shape[1] // parts,))
+        self.right = right
+
+    def take(self, bit):
+        part = Product.__new__(Product)
+        part.left = pick(self.left, bit, self.left.ndim - 2)
+        part.right = self.right
+        return part
+
+    def value(self):
+        return t_dot(self.left, self.right)
+
+
+class Ready:
+    def __init__(self, values, parts):
+        bits = int(math.log2(parts))
+        self.values = values.reshape(
+            (2,) * bits + (values.shape[0] // parts, values.shape[1])
+        )
+
+    def take(self, bit):
+        part = Ready.__new__(Ready)
+        part.values = pick(self.values, bit, self.values.ndim - 3)
+        return part
+
+    def value(self):
+        return self.values
+
+
+def reduce_rows(terms):
+    received = []
+    for bit in range(bit_count("fsdp")):
+        mine = own_bit("fsdp", bit)
+        send = jnp.concatenate([term.take(1 - mine).value() for term in terms], axis=-1)
+        for item in received:
+            send = send + pick(item, 1 - mine, item.ndim - 3).astype(jnp.float32)
+        terms = [term.take(mine) for term in terms]
+        received = [pick(item, mine, item.ndim - 3) for item in received]
+        received.append(swap(rounded(send), "fsdp", bit))
+    total = jnp.concatenate([term.value() for term in terms], axis=-1)
+    for item in received:
+        total = total + item.astype(jnp.float32)
+    total = rounded(total)
+    for bit in range(bit_count("ctx")):
+        mine = own_bit("ctx", bit)
+        halves = total.reshape(2, total.shape[0] // 2, total.shape[1])
+        other = swap(pick(halves, 1 - mine, 0), "ctx", bit)
+        total = rounded(pick(halves, mine, 0).astype(jnp.float32) + other.astype(jnp.float32))
+    for bit in reversed(range(bit_count("ctx"))):
+        mine = own_bit("ctx", bit)
+        other = swap(total, "ctx", bit)
+        total = jnp.where(
+            mine == 0,
+            jnp.concatenate([total, other], axis=0),
+            jnp.concatenate([other, total], axis=0),
+        )
+    return total
 
 
 def body(tokens, encoded, cotangent, w_self, w_cross, w_ffn, gains, table, bucket_ids, block_order):
@@ -336,11 +423,18 @@
     seq_length = bucket_ids.shape[0]
     steps = seq_length // block
     ctx_place = lax.axis_index("ctx")
-    table_rows = lax.all_gather(table, "fsdp", axis=0, tiled=True)
-    gain_rows = lax.all_gather(gains, "fsdp", axis=1, tiled=True)
-    whole_self = lax.all_gather(w_self, "fsdp", axis=0, tiled=True)
-    whole_cross = lax.all_gather(w_cross, "fsdp", axis=0, tiled=True)
-    whole_ffn = lax.all_gather(w_ffn, "fsdp", axis=0, tiled=True)
+    fsdp_size = lax.axis_size("fsdp")
+    small = lax.all_gather(
+        jnp.concatenate([gains.reshape(1, -1), table.reshape(1, -1)], axis=1),
+        "fsdp", axis=0, tiled=True,
+    )
+    gain_rows = jnp.transpose(
+        small[:, : gains.size].reshape((fsdp_size,) + gains.shape), (1, 0, 2)
+    ).reshape(gains.shape[0], -1)
+    table_rows = small[:, gains.size :].reshape(-1, head_count)
+    whole_self = gather_rows(w_self)
+    whole_cross = gather_rows(w_cross)
+    whole_ffn = gather_rows(w_ffn)
     gain_float = gain_rows.astype(jnp.float32)
     bucket_count = table_rows.shape[0]
     in_bucket = (
@@ -384,14 +478,11 @@
     grad_mixed = dot(grad_branch_three, whole_ffn[:, 2 * hidden_units :])
     grad_gate_up = rounded(gated_back(grad_mixed)[0])
     grad_normed_three = dot_t(grad_gate_up, whole_ffn[:, : 2 * hidden_units])
-    ffn_grad = reduce_weight(
-        jnp.concatenate(
-            [
-                rounded(t_dot(normed_three, grad_gate_up)),
-                rounded(t_dot(grad_branch_three, mixed_rows)),
-            ],
-            axis=1,
-        )
+    ffn_grad = reduce_rows(
+        [
+            Product(normed_three, grad_gate_up, fsdp_size),
+            Product(grad_branch_three, mixed_rows, fsdp_size),
+        ]
     )
     norm_part, gain_three = jax.vjp(row_norm, after_two, gain_float[2])[1](grad_normed_three)
     grad_after_one = grad_after_two + norm_part
@@ -402,6 +493,12 @@
         head_size,
     )
     encoder_own = lax.psum_scatter(encoder_full, "ctx", scatter_dimension=1, tiled=True)
+    cross_grad = reduce_rows(
+        [
+            Product(normed_two, grad_cross_query, fsdp_size),
+            Product(cross_rows, grad_branch_two, fsdp_size),
+        ]
+    )
     grad_normed_two = dot_t(grad_cross_query, whole_cross[:, :model_width])
     norm_part, gain_two = jax.vjp(row_norm, after_one, gain_float[1])[1](grad_normed_two)
     grad_inputs_one = grad_after_one + norm_part
@@ -416,47 +513,58 @@
     grad_encoded = rounded(
         dot_t(grad_encoder_kv, whole_cross[:, model_width : 3 * model_width])
     )
-    cross_grad = reduce_weight(
-        jnp.concatenate(
-            [
-                rounded(t_dot(normed_two, grad_cross_query)),
-                rounded(t_dot(encoder_rows, grad_encoder_kv)),
-                rounded(t_dot(cross_rows, grad_branch_two)),
-            ],
-            axis=1,
-        )
-    )
+    encoder_grad = reduce_rows([Product(encoder_rows, grad_encoder_kv, fsdp_size)])
     grad_table = lax.dot_general(
         in_bucket,
         by_distance_sums(distance_sums, block),
         (((1,), (1,)), ((), ())),
         precision=lax.Precision.HIGHEST,
     )
+    query_grad = reduce_rows(
+        [
+            Product(normed_one, grad_query, fsdp_size),
+            Product(attended, grad_branch_one, fsdp_size),
+        ]
+    )
     grad_projected = jnp.concatenate([grad_query, grad_key_own[0], grad_key_own[1]], axis=1)
     grad_normed_one = dot_t(grad_projected, whole_self[:, : 3 * model_width])
-    self_grad = reduce_weight(
+    norm_part, gain_one = jax.vjp(row_norm, inputs, gain_float[0])[1](grad_normed_one)
+    grad_tokens = rounded(grad_inputs_one + norm_part)
+    gain_columns = jnp.stack([gain_one, gain_two, gain_three], axis=1)
+    table_columns = jnp.pad(
+        grad_table.reshape(fsdp_size, -1, head_count),
+        ((0, 0), (0, gains.shape[1] - table.shape[0]), (0, 0)),
+    ).reshape(model_width, head_count)
+    small_columns = jnp.pad(
+        jnp.concatenate([gain_columns, table_columns], axis=1),
+        ((0, 0), (0, LANES - gains.shape[0] - head_count)),
+    )
+    key_grad = reduce_rows(
+        [
+            Product(normed_one, grad_projected[:, model_width:], fsdp_size),
+            Ready(small_columns, fsdp_size),
+        ]
+    )
+    wide = lambda values: values.astype(jnp.float32)
+    self_grad = wide(
         jnp.concatenate(
             [
-                rounded(t_dot(normed_one, grad_projected)),
-                rounded(t_dot(attended, grad_branch_one)),
+                query_grad[:, :model_width],
+                key_grad[:, : 2 * model_width],
+                query_grad[:, model_width:],
             ],
             axis=1,
         )
     )
-    norm_part, gain_one = jax.vjp(row_norm, inputs, gain_float[0])[1](grad_normed_one)
-    grad_tokens = rounded(grad_inputs_one + norm_part)
-    gain_terms = jnp.stack([gain_one, gain_two, gain_three])
-    small = jnp.concatenate([gain_terms.reshape(-1), grad_table.reshape(-1)])
-    small = lax.psum(small, ("fsdp", "ctx"))
-    fsdp_place = lax.axis_index("fsdp")
-    gain_total = small[: gain_terms.size].reshape(gain_terms.shape)
-    table_total = small[gain_terms.size :].reshape(grad_table.shape)
-    gain_own = lax.dynamic_slice_in_dim(
-        gain_total, fsdp_place * gains.shape[1], gains.shape[1], axis=1
-    )
-    table_own = lax.dynamic_slice_in_dim(
-        table_total, fsdp_place * table.shape[0], table.shape[0], axis=0
-    )
+    cross_grad = wide(
+        jnp.concatenate(
+            [cross_grad[:, :model_width], encoder_grad, cross_grad[:, model_width:]], axis=1
+        )
+    )
+    ffn_grad = wide(ffn_grad)
+    small_own = wide(key_grad[:, 2 * model_width :])
+    gain_own = jnp.transpose(small_own[:, : gains.shape[0]])
+    table_own = small_own[: table.shape[0], gains.shape[0] : gains.shape[0] + head_count]
     return (
         output[None],
         grad_tokens[None],

time: 1050 us -> 650 us (0.62)
  waiting for transfers between devices: 789 us -> 306 us
  starting transfers between devices: 1 us -> 38.3 us
  local copies, waits for them, and re-layouts: 18.6 us -> 52.2 us
  blocking collectives: 51.8 us -> 25.5 us
  other arithmetic: 22.8 us -> 40.1 us
  matrix products: 55.6 us -> 69.5 us
    reduce_scatter x3 -> x0, waiting for transfers between devices: 355 us -> none  [reduce_weight(): lax.psum_scatter(rounded(grad), ('fsdp', 'ctx'), scatter_dimension=0, til...]
    ppermute x0 -> x49, waiting for transfers between devices: none -> 268 us  [swap(): lax.ppermute(values, axis_name, [(i, i ^ 1 << bit) for i in range(size)])]
    all_gather x6 -> x0, waiting for transfers between devices: 198 us -> none  [the longest x3 77 us: reduce_weight(): return lax.all_gather(share, 'ctx', axis=0, tiled=True).astype(jnp.float32)]
    reduce_scatter x1, waiting for transfers between devices: 97.2 us -> 0.01 us  [body(): lax.psum_scatter(grad_key_full, 'ctx', scatter_dimension=1, tiled=True)]
    all_gather x1, waiting for transfers between devices: 83.5 us -> 0.29 us  [body(): lax.all_gather(projected[:, model_width:], 'ctx', axis=0, tiled=True)]
    psum x1 -> x0, blocking collectives: 40.6 us -> none  [body(): small = lax.psum(small, ('fsdp', 'ctx'))]
    ppermute x0 -> x49, starting transfers between devices: none -> 38 us  [swap(): lax.ppermute(values, axis_name, [(i, i ^ 1 << bit) for i in range(size)])]
    dynamic_update_slice x0 -> x12, local copies, waits for them, and re-layouts: none -> 17.6 us  [gather_rows(): whole = lax.dynamic_update_slice_in_dim(whole, piece, at * rows, 0)]
  transfers between devices with their start and end apart: 13 -> 53, of which waited for: 12 -> 32; matrix products, arithmetic and copies ran while one was open for 7% -> 20% of each run, Pallas kernels for 8% -> 12%
where the time goes in v2:
time: 650 us; the launch traced here: 644 us
  waiting for transfers between devices  306 us (47%)
  Pallas kernels  97.1 us (15%)
  matrix products  69.5 us (11%)
  local copies, waits for them, and re-layouts  52.2 us (8%)
  other arithmetic  40.1 us (6%)
  starting transfers between devices  38.3 us (6%)
  blocking collectives  25.5 us (4%)
  between operations  15.4 us (2%)
    ppermute x49, waiting for transfers between devices, swap(): lax.ppermute(values, axis_name, [(i, i ^ 1 << bit) for i in range(size)])  268 us
    pallas_call x2, Pallas kernels, attention_backward(): pl.pallas_call(functools.partial(backward_kernel, head_size, biased), gri...  60.9 us
    ppermute x49, starting transfers between devices, swap(): lax.ppermute(values, axis_name, [(i, i ^ 1 << bit) for i in range(size)])  38 us
    all_gather x1, waiting for transfers between devices, body(): encoder_kv = lax.all_gather(encoder_local, 'ctx', axis=0, tiled=True)  37.4 us
    dot_general x24, matrix products, t_dot(): lax.dot_general(left, right, (((0,), (0,)), ((), ())), preferred_element_...  29.9 us
    pallas_call x2, Pallas kernels, attention_forward(): pl.pallas_call(functools.partial(forward_kernel, head_size, tiles is not...  29.6 us
    all_gather x1, blocking collectives, body(): lax.all_gather(jnp.concatenate([gains.reshape(1, -1), table.reshape(1, -1...  25.5 us
    dot_general x7, matrix products, dot_t(): lax.dot_general(left, right, (((1,), (1,)), ((), ())), preferred_element_...  20.3 us
  transfers between devices with their start and end apart: 53, of which 32 were waited for; matrix products, arithmetic and copies ran while one was open for 20% of the time, Pallas kernels for 12%

profile of v2, /device:TPU:0, one launch (start us, length us, event | category | flops | bytes accessed | tf_op | source)
XLA Modules:
  0.0 644.0 jit_solution(3364835588655552472)
XLA Ops:
  11.8 25.5 %all-gather = bf16[4,1,672]{2,1,0:T(2,128)(2,1)S(1)} all-gather(bf16[1,1,672]{2,1,0:T(2,128)(2,1)S(1)} %maximum_bitcast_fusion), channel_id=1, replica_groups=mesh['ctx'=8,'fsdp'=4] {'fsdp'}, dimensions={0}, use_global_device_ids=true | all-gather | bytes 6720 | tf_op jit(solution)/shard_map/all_gather | solution.py:427
  48.6 26.5 %collective-permute-done.3 = bf16[192,3072]{1,0:T(8,128)(2,1)} collective-permute-done((bf16[192,3072]{1,0:T(8,128)(2,1)S(1)}, bf16[192,3072]{1,0:T(8,128)(2,1)}, u32[]{:S(2)}, u32[]{:S(2)}) %collective-permute-start.3) | collective-permute-done | bytes 1179680 | tf_op jit(solution)/shard_map/ppermute | solution.py:331
  88.5 6.7 %bias_tiles.1.refs_4_ = bf16[12,17,128,128]{3,2,1,0:T(8,128)(2,1)} custom-call(f32[12,17,256]{2,1,0:T(8,128)} %select_maximum_fusion.3.vector_ref), custom_call_target="tpu_custom_call" | custom-call | tf_op jit(solution)/shard_map/bias_tiles/pallas_call | solution.py:57
  97.2 31.9 %collective-permute-done.6 = bf16[192,6144]{1,0:T(8,128)(2,1)} collective-permute-done((bf16[192,6144]{1,0:T(8,128)(2,1)}, bf16[192,6144]{1,0:T(8,128)(2,1)}, u32[]{:S(2)}, u32[]{:S(2)}) %collective-permute-start.6) | collective-permute-done | bytes 2359328 | tf_op jit(solution)/shard_map/ppermute | solution.py:331
  129.6 4.8 broadcast_in_dim.42
  146.9 18.6 %attention_forward.2 = (bf16[256,768]{1,0:T(8,128)(2,1)}, bf16[12,256,2048]{2,1,0:T(8,128)(2,1)}, f32[12,256,128]{2,1,0:T(8,128)}) custom-call(s32[32]{0:T(128)} %compare_select_fusion.refs_0_, bf16[256,768]{1,0:T(8,128)(2,1)} %slice.158.refs_1_, bf16[2048,1536]{1,0:T(8,128)(2,1)} %all-gather.4.cloned.1.call-done.refs_2_.refs_3_, ...), custom_call_target="tpu_custom_call" | custom-call | flops 3221225472 | bytes 18874368 | tf_op jit(solution)/shard_map/attention_forward/pallas_call | solution.py:139
  171.1 37.4 %all-gather.6.cloned.1.call-done.refs_1_.refs_2_ = bf16[1024,1536]{1,0:T(8,128)(2,1)} async-done(((bf16[128,1536]{1,0:T(8,128)(2,1)}), bf16[1024,1536]{1,0:T(8,128)(2,1)}) %all-gather.6.cloned.1.call-update) | async-done | bytes 3145744 | tf_op jit(solution)/shard_map/all_gather | solution.py:461
  208.4 11.0 %attention_forward.3 = (bf16[256,768]{1,0:T(8,128)(2,1)}, bf16[12,256,1024]{2,1,0:T(8,128)(2,1)}, f32[12,256,128]{2,1,0:T(8,128)}) custom-call(bf16[256,768]{1,0:T(8,128)(2,1)} %convolution_convert_fusion.12.refs_0_, bf16[1024,1536]{1,0:T(8,128)(2,1)} %all-gather.6.cloned.1.call-done.refs_1_.refs_2_, ...), custom_call_target="tpu_custom_call" | custom-call | flops 1610612736 | bytes 9437184 | tf_op jit(solution)/shard_map/attention_forward/pallas_call | solution.py:139
  221.5 4.7 fusion.2
  226.3 5.2 fusion.82
  231.8 4.9 multiply_reduce_fusion
  238.3 11.6 %attention_backward.2 = (bf16[256,768]{1,0:T(8,128)(2,1)}, bf16[2,1024,768]{2,1,0:T(8,128)(2,1)}) custom-call(bf16[256,768]{1,0:T(8,128)(2,1)} %convolution_convert_fusion.12.refs_0_, bf16[1024,1536]{1,0:T(8,128)(2,1)} %all-gather.6.cloned.1.call-done.refs_1_.refs_2_, bf16[1024,1536]{1,0:T(8,128)(2,1)} %all-gather.6.cloned.1.call-done.refs_1_.refs_2_, ...), custom_call_target="tpu_custom_call" | custom-call | flops 3221225472 | bytes 12582912 | tf_op jit(solution)/shard_map/attention_backward/pallas_call | solution.py:268
  267.7 49.3 %attention_backward.3 = (bf16[256,768]{1,0:T(8,128)(2,1)}, bf16[2,2048,768]{2,1,0:T(8,128)(2,1)}, f32[12,16,256]{2,1,0:T(8,128)}) custom-call(s32[32]{0:T(128)} %compare_select_fusion.refs_0_, bf16[256,768]{1,0:T(8,128)(2,1)} %slice.158.refs_1_, bf16[2048,1536]{1,0:T(8,128)(2,1)} %all-gather.4.cloned.1.call-done.refs_2_.refs_3_, ...), custom_call_target="tpu_custom_call" | custom-call | flops 6442450944 | bytes 25165824 | tf_op jit(solution)/shard_map/attention_backward/pallas_call | solution.py:268
  347.2 4.0 fusion.39
  359.0 9.6 %collective-permute-done.10 = bf16[192,1536]{1,0:T(8,128)(2,1)S(1)} collective-permute-done((bf16[192,1536]{1,0:T(8,128)(2,1)S(1)}, bf16[192,1536]{1,0:T(8,128)(2,1)S(1)}, u32[]{:S(2)}, u32[]{:S(2)}) %collective-permute-start.10) | collective-permute-done | bytes 589856 | tf_op jit(solution)/shard_map/ppermute | solution.py:331
  370.5 10.3 %collective-permute-done.26 = bf16[192,1536]{1,0:T(8,128)(2,1)S(1)} collective-permute-done((bf16[192,1536]{1,0:T(8,128)(2,1)S(1)}, bf16[192,1536]{1,0:T(8,128)(2,1)S(1)}, u32[]{:S(2)}, u32[]{:S(2)}) %collective-permute-start.26) | collective-permute-done | bytes 589856 | tf_op jit(solution)/shard_map/ppermute | solution.py:331
  387.5 5.0 collective-permute-done.27
  394.1 7.2 %collective-permute-done.12 = bf16[48,1536]{1,0:T(8,128)(2,1)S(1)} collective-permute-done((bf16[48,1536]{1,0:T(8,128)(2,1)S(1)}, bf16[48,1536]{1,0:T(8,128)(2,1)S(1)}, u32[]{:S(2)}, u32[]{:S(2)}) %collective-permute-start.12) | collective-permute-done | bytes 147488 | tf_op jit(solution)/shard_map/ppermute | solution.py:331
  401.4 6.6 %collective-permute-done.28 = bf16[48,1536]{1,0:T(8,128)(2,1)S(1)} collective-permute-done((bf16[48,1536]{1,0:T(8,128)(2,1)S(1)}, bf16[48,1536]{1,0:T(8,128)(2,1)S(1)}, u32[]{:S(2)}, u32[]{:S(2)}) %collective-permute-start.28) | collective-permute-done | bytes 147488 | tf_op jit(solution)/shard_map/ppermute | solution.py:331
  411.2 4.9 collective-permute-done.29
  438.8 10.0 %collective-permute-done.32 = bf16[96,1536]{1,0:T(8,128)(2,1)S(1)} collective-permute-done((bf16[96,1536]{1,0:T(8,128)(2,1)S(1)}, bf16[96,1536]{1,0:T(8,128)(2,1)S(1)}, u32[]{:S(2)}, u32[]{:S(2)}) %collective-permute-start.32) | collective-permute-done | bytes 294944 | tf_op jit(solution)/shard_map/ppermute | solution.py:331
  450.1 48.0 %collective-permute-done.34 = bf16[192,1536]{1,0:T(8,128)(2,1)S(1)} collective-permute-done((bf16[192,1536]{1,0:T(8,128)(2,1)S(1)}, bf16[192,1536]{1,0:T(8,128)(2,1)S(1)}, u32[]{:S(2)}, u32[]{:S(2)}) %collective-permute-start.34) | collective-permute-done | bytes 589856 | tf_op jit(solution)/shard_map/ppermute | solution.py:331
  502.5 4.8 collective-permute-done.35
  508.4 4.2 collective-permute-done.36
  515.0 4.7 collective-permute-done.37
  519.9 14.4 %collective-permute-done.43 = bf16[96,6144]{1,0:T(8,128)(2,1)S(1)} collective-permute-done((bf16[96,6144]{1,0:T(8,128)(2,1)S(1)}, bf16[96,6144]{1,0:T(8,128)(2,1)S(1)}, u32[]{:S(2)}, u32[]{:S(2)}) %collective-permute-start.43) | collective-permute-done | bytes 1179680 | tf_op jit(solution)/shard_map/ppermute | solution.py:331
  555.8 11.2 %collective-permute-done.45 = bf16[24,6144]{1,0:T(8,128)(2,1)S(1)} collective-permute-done((bf16[24,6144]{1,0:T(8,128)(2,1)S(1)}, bf16[24,6144]{1,0:T(8,128)(2,1)S(1)}, u32[]{:S(2)}, u32[]{:S(2)}) %collective-permute-start.45) | collective-permute-done | bytes 294944 | tf_op jit(solution)/shard_map/ppermute | solution.py:331
  570.7 11.2 %collective-permute-done.46 = bf16[24,6144]{1,0:T(8,128)(2,1)S(1)} collective-permute-done((bf16[24,6144]{1,0:T(8,128)(2,1)S(1)}, bf16[24,6144]{1,0:T(8,128)(2,1)S(1)}, u32[]{:S(2)}, u32[]{:S(2)}) %collective-permute-start.46) | collective-permute-done | bytes 294944 | tf_op jit(solution)/shard_map/ppermute | solution.py:331
  584.3 14.0 %collective-permute-done.47 = bf16[48,6144]{1,0:T(8,128)(2,1)S(1)} collective-permute-done((bf16[48,6144]{1,0:T(8,128)(2,1)S(1)}, bf16[48,6144]{1,0:T(8,128)(2,1)S(1)}, u32[]{:S(2)}, u32[]{:S(2)}) %collective-permute-start.47) | collective-permute-done | bytes 589856 | tf_op jit(solution)/shard_map/ppermute | solution.py:331
  602.3 4.1 collective-permute-done.21
  612.0 12.2 %collective-permute-done.48 = bf16[96,6144]{1,0:T(8,128)(2,1)S(1)} collective-permute-done((bf16[96,6144]{1,0:T(8,128)(2,1)S(1)}, bf16[96,6144]{1,0:T(8,128)(2,1)S(1)}, u32[]{:S(2)}, u32[]{:S(2)}) %collective-permute-start.48) | collective-permute-done | bytes 1179680 | tf_op jit(solution)/shard_map/ppermute | solution.py:331
  629.8 4.2 collective-permute-done.24
  (366 shorter events, 200.0 us)
Async XLA Ops:
  7.2 139.7 %all-gather.4.cloned.1.call-start = ((), (), s32[]{:S(2)}) async-start(), calls=%async_computation.2 | async-start | bytes 7077888 | tf_op jit(solution)/shard_map/all_gather | solution.py:459
  7.2 31.4 %collective-permute-start = (bf16[192,3072]{1,0:T(8,128)(2,1)}, bf16[192,3072]{1,0:T(8,128)(2,1)S(1)}, u32[]{:S(2)}, u32[]{:S(2)}) collective-permute-start(bf16[192,3072]{1,0:T(8,128)(2,1)} %param.13), channel_id=1, source_target_pairs={{0,2},{1,3},{2,0},{3,1},{4,6},{5,7},{6,4},{7,5},{8,10},{9,11},{10,... | collective-permute-start | bytes 3538952 | tf_op jit(solution)/shard_map/ppermute | solution.py:331
  10.2 30.5 %collective-permute-start.1 = (bf16[192,3072]{1,0:T(8,128)(2,1)}, bf16[192,3072]{1,0:T(8,128)(2,1)S(1)}, u32[]{:S(2)}, u32[]{:S(2)}) collective-permute-start(bf16[192,3072]{1,0:T(8,128)(2,1)} %param.13), channel_id=1, source_target_pairs={{0,1},{1,0},{2,3},{3,2},{4,5},{5,4},{6,7},{7,6},{8,9},{9,8},{10,11... | collective-permute-start | bytes 3538952 | tf_op jit(solution)/shard_map/ppermute | solution.py:331
  46.2 162.2 %all-gather.6.cloned.1.call-start = ((), (), s32[]{:S(2)}) async-start(), calls=%async_computation.3 | async-start | bytes 3538944 | tf_op jit(solution)/shard_map/all_gather | solution.py:461
  46.8 28.3 %collective-permute-start.3 = (bf16[192,3072]{1,0:T(8,128)(2,1)S(1)}, bf16[192,3072]{1,0:T(8,128)(2,1)}, u32[]{:S(2)}, u32[]{:S(2)}) collective-permute-start(bf16[192,3072]{1,0:T(8,128)(2,1)S(1)} %copy-done.37), channel_id=1, source_target_pairs={{0,2},{1,3},{2,0},{3,1},{4,6},{5,7},{6,4},{7,5},{8,10},{9,11},{10,... | collective-permute-start | bytes 3538952 | tf_op jit(solution)/shard_map/ppermute | solution.py:331
  48.6 30.9 %collective-permute-start.4 = (bf16[192,3072]{1,0:T(8,128)(2,1)S(1)}, bf16[192,3072]{1,0:T(8,128)(2,1)}, u32[]{:S(2)}, u32[]{:S(2)}) collective-permute-start(bf16[192,3072]{1,0:T(8,128)(2,1)S(1)} %copy-done.37), channel_id=1, source_target_pairs={{0,1},{1,0},{2,3},{3,2},{4,5},{5,4},{6,7},{7,6},{8,9},{9,8},{10,11... | collective-permute-start | bytes 3538952 | tf_op jit(solution)/shard_map/ppermute | solution.py:331
  75.1 54.0 %collective-permute-start.6 = (bf16[192,6144]{1,0:T(8,128)(2,1)}, bf16[192,6144]{1,0:T(8,128)(2,1)}, u32[]{:S(2)}, u32[]{:S(2)}) collective-permute-start(bf16[192,6144]{1,0:T(8,128)(2,1)} %param.15), channel_id=1, source_target_pairs={{0,2},{1,3},{2,0},{3,1},{4,6},{5,7},{6,4},{7,5},{8,10},{9,11},{10,... | collective-permute-start | bytes 7077896 | tf_op jit(solution)/shard_map/ppermute | solution.py:331
  76.9 64.9 %collective-permute-start.7 = (bf16[192,6144]{1,0:T(8,128)(2,1)}, bf16[192,6144]{1,0:T(8,128)(2,1)}, u32[]{:S(2)}, u32[]{:S(2)}) collective-permute-start(bf16[192,6144]{1,0:T(8,128)(2,1)} %param.15), channel_id=1, source_target_pairs={{0,1},{1,0},{2,3},{3,2},{4,5},{5,4},{6,7},{7,6},{8,9},{9,8},{10,11... | collective-permute-start | bytes 7077896 | tf_op jit(solution)/shard_map/ppermute | solution.py:331
  85.7 340.8 %reduce-scatter.5.cloned.1.call-start = ((), (), s32[]{:S(2)}) async-start(), calls=%async_computation.5 | async-start | bytes 3538944 | tf_op jit(solution)/shard_map/reduce_scatter | solution.py:495
  129.1 15.9 %collective-permute-start.8 = (bf16[192,6144]{1,0:T(8,128)(2,1)}, bf16[192,6144]{1,0:T(8,128)(2,1)S(1)}, u32[]{:S(2)}, u32[]{:S(2)}) collective-permute-start(bf16[192,6144]{1,0:T(8,128)(2,1)} %collective-permute-done.6), channel_id=1, source_target_pairs={{0,1},{1,0},{2,3},{3,2},{4,5},{5,4},{6,7},{7,6},{8,9},{9,8},{10,11... | collective-permute-start | bytes 7077896 | tf_op jit(solution)/shard_map/ppermute | solution.py:331
  252.6 290.3 %reduce-scatter.3.cloned.1.call-start = ((), (), s32[]{:S(2)}) async-start(), calls=%async_computation.4 | async-start | bytes 7077888 | tf_op jit(solution)/shard_map/reduce_scatter | solution.py:510
  319.5 31.7 %collective-permute-start.9 = (bf16[2,192,1536]{2,1,0:T(8,128)(2,1)}, bf16[2,192,1536]{2,1,0:T(8,128)(2,1)}, u32[]{:S(2)}, u32[]{:S(2)}) collective-permute-start(bf16[2,192,1536]{2,1,0:T(8,128)(2,1)} %pad_maximum_fusion.2), channel_id=1, source_target_pairs={{0,1},{1,0},{2,3},{3,2},{4,5},{5,4},{6,7},{7,6},{8,9},{9,8},{10,11... | collective-permute-start | bytes 3538952 | tf_op jit(solution)/shard_map/ppermute | solution.py:331
  325.6 31.6 %collective-permute-start.25 = (bf16[2,192,1536]{2,1,0:T(8,128)(2,1)}, bf16[2,192,1536]{2,1,0:T(8,128)(2,1)}, u32[]{:S(2)}, u32[]{:S(2)}) collective-permute-start(bf16[2,192,1536]{2,1,0:T(8,128)(2,1)} %pad_maximum_fusion.3), channel_id=1, source_target_pairs={{0,1},{1,0},{2,3},{3,2},{4,5},{5,4},{6,7},{7,6},{8,9},{9,8},{10,11... | collective-permute-start | bytes 3538952 | tf_op jit(solution)/shard_map/ppermute | solution.py:331
  330.3 98.8 %collective-permute-start.41 = (bf16[2,192,6144]{2,1,0:T(8,128)(2,1)}, bf16[2,192,6144]{2,1,0:T(8,128)(2,1)}, u32[]{:S(2)}, u32[]{:S(2)}) collective-permute-start(bf16[2,192,6144]{2,1,0:T(8,128)(2,1)} %pad_maximum_fusion), channel_id=1, source_target_pairs={{0,1},{1,0},{2,3},{3,2},{4,5},{5,4},{6,7},{7,6},{8,9},{9,8},{10,11... | collective-permute-start | bytes 14155784 | tf_op jit(solution)/shard_map/ppermute | solution.py:331
  352.4 16.2 %collective-permute-start.10 = (bf16[192,1536]{1,0:T(8,128)(2,1)S(1)}, bf16[192,1536]{1,0:T(8,128)(2,1)S(1)}, u32[]{:S(2)}, u32[]{:S(2)}) collective-permute-start(bf16[192,1536]{1,0:T(8,128)(2,1)S(1)} %fusion.49), channel_id=1, source_target_pairs={{0,2},{1,3},{2,0},{3,1},{4,6},{5,7},{6,4},{7,5},{8,10},{9,11},{10,... | collective-permute-start | bytes 1769480 | tf_op jit(solution)/shard_map/ppermute | solution.py:331
  358.6 22.2 %collective-permute-start.26 = (bf16[192,1536]{1,0:T(8,128)(2,1)S(1)}, bf16[192,1536]{1,0:T(8,128)(2,1)S(1)}, u32[]{:S(2)}, u32[]{:S(2)}) collective-permute-start(bf16[192,1536]{1,0:T(8,128)(2,1)S(1)} %fusion.52), channel_id=1, source_target_pairs={{0,2},{1,3},{2,0},{3,1},{4,6},{5,7},{6,4},{7,5},{8,10},{9,11},{10,... | collective-permute-start | bytes 1769480 | tf_op jit(solution)/shard_map/ppermute | solution.py:331
  369.9 15.5 %collective-permute-start.11 = (bf16[96,1536]{1,0:T(8,128)(2,1)S(1)}, bf16[96,1536]{1,0:T(8,128)(2,1)S(1)}, u32[]{:S(2)}, u32[]{:S(2)}) collective-permute-start(bf16[96,1536]{1,0:T(8,128)(2,1)S(1)} %dynamic-slice_bitcast_fusion.6), channel_id=1, source_target_pairs={{0,4},{4,0},{8,12},{12,8},{16,20},{20,16},{24,28},{28,24},{1,5},{5... | collective-permute-start | bytes 884744 | tf_op jit(solution)/shard_map/ppermute | solution.py:331
  385.5 15.8 %collective-permute-start.12 = (bf16[48,1536]{1,0:T(8,128)(2,1)S(1)}, bf16[48,1536]{1,0:T(8,128)(2,1)S(1)}, u32[]{:S(2)}, u32[]{:S(2)}) collective-permute-start(bf16[48,1536]{1,0:T(8,128)(2,1)S(1)} %dynamic-slice_bitcast_fusion.10), channel_id=1, source_target_pairs={{0,8},{4,12},{8,0},{12,4},{16,24},{20,28},{24,16},{28,20},{1,9},{5... | collective-permute-start | bytes 442376 | tf_op jit(solution)/shard_map/ppermute | solution.py:331
  392.6 15.4 %collective-permute-start.28 = (bf16[48,1536]{1,0:T(8,128)(2,1)S(1)}, bf16[48,1536]{1,0:T(8,128)(2,1)S(1)}, u32[]{:S(2)}, u32[]{:S(2)}) collective-permute-start(bf16[48,1536]{1,0:T(8,128)(2,1)S(1)} %dynamic-slice_bitcast_fusion.9), channel_id=1, source_target_pairs={{0,8},{4,12},{8,0},{12,4},{16,24},{20,28},{24,16},{28,20},{1,9},{5... | collective-permute-start | bytes 442376 | tf_op jit(solution)/shard_map/ppermute | solution.py:331
  431.7 67.6 %collective-permute-start.42 = (bf16[192,6144]{1,0:T(8,128)(2,1)S(1)}, bf16[192,6144]{1,0:T(8,128)(2,1)S(1)}, u32[]{:S(2)}, u32[]{:S(2)}) collective-permute-start(bf16[192,6144]{1,0:T(8,128)(2,1)S(1)} %fusion.6), channel_id=1, source_target_pairs={{0,2},{1,3},{2,0},{3,1},{4,6},{5,7},{6,4},{7,5},{8,10},{9,11},{10,... | collective-permute-start | bytes 7077896 | tf_op jit(solution)/shard_map/ppermute | solution.py:331
  438.3 59.8 %collective-permute-start.34 = (bf16[192,1536]{1,0:T(8,128)(2,1)S(1)}, bf16[192,1536]{1,0:T(8,128)(2,1)S(1)}, u32[]{:S(2)}, u32[]{:S(2)}) collective-permute-start(bf16[192,1536]{1,0:T(8,128)(2,1)S(1)} %fusion.54), channel_id=1, source_target_pairs={{0,2},{1,3},{2,0},{3,1},{4,6},{5,7},{6,4},{7,5},{8,10},{9,11},{10,... | collective-permute-start | bytes 1769480 | tf_op jit(solution)/shard_map/ppermute | solution.py:331
  507.7 26.5 %collective-permute-start.43 = (bf16[96,6144]{1,0:T(8,128)(2,1)S(1)}, bf16[96,6144]{1,0:T(8,128)(2,1)S(1)}, u32[]{:S(2)}, u32[]{:S(2)}) collective-permute-start(bf16[96,6144]{1,0:T(8,128)(2,1)S(1)} %dynamic-slice_bitcast_fusion), channel_id=1, source_target_pairs={{0,4},{4,0},{8,12},{12,8},{16,20},{20,16},{24,28},{28,24},{1,5},{5... | collective-permute-start | bytes 3538952 | tf_op jit(solution)/shard_map/ppermute | solution.py:331
  519.8 14.8 %collective-permute-start.38 = (bf16[24,1536]{1,0:T(8,128)(2,1)S(1)}, bf16[24,1536]{1,0:T(8,128)(2,1)S(1)}, u32[]{:S(2)}, u32[]{:S(2)}) collective-permute-start(bf16[24,1536]{1,0:T(8,128)(2,1)S(1)} %fusion.121), channel_id=1, source_target_pairs={{0,16},{4,20},{8,24},{12,28},{16,0},{20,4},{24,8},{28,12},{1,17},{... | collective-permute-start | bytes 221192 | tf_op jit(solution)/shard_map/ppermute | solution.py:331
  537.3 14.4 %collective-permute-start.44 = (bf16[48,6144]{1,0:T(8,128)(2,1)}, bf16[48,6144]{1,0:T(8,128)(2,1)}, u32[]{:S(2)}, u32[]{:S(2)}) collective-permute-start(bf16[48,6144]{1,0:T(8,128)(2,1)} %dynamic-slice_bitcast_fusion.1), channel_id=1, source_target_pairs={{0,8},{4,12},{8,0},{12,4},{16,24},{20,28},{24,16},{28,20},{1,9},{5... | collective-permute-start | bytes 1769480 | tf_op jit(solution)/shard_map/ppermute | solution.py:331
  542.2 58.7 %collective-permute-start.40 = (bf16[96,1536]{1,0:T(8,128)(2,1)}, bf16[96,1536]{1,0:T(8,128)(2,1)}, u32[]{:S(2)}, u32[]{:S(2)}) collective-permute-start(bf16[96,1536]{1,0:T(8,128)(2,1)} %maximum_select_fusion.10), channel_id=1, source_target_pairs={{0,4},{4,0},{8,12},{12,8},{16,20},{20,16},{24,28},{28,24},{1,5},{5... | collective-permute-start | bytes 884744 | tf_op jit(solution)/shard_map/ppermute | solution.py:331
  553.0 14.0 %collective-permute-start.45 = (bf16[24,6144]{1,0:T(8,128)(2,1)S(1)}, bf16[24,6144]{1,0:T(8,128)(2,1)S(1)}, u32[]{:S(2)}, u32[]{:S(2)}) collective-permute-start(bf16[24,6144]{1,0:T(8,128)(2,1)S(1)} %dynamic-slice_bitcast_fusion.3), channel_id=1, source_target_pairs={{0,16},{4,20},{8,24},{12,28},{16,0},{20,4},{24,8},{28,12},{1,17},{... | collective-permute-start | bytes 884744 | tf_op jit(solution)/shard_map/ppermute | solution.py:331
  554.2 15.5 %collective-permute-start.18 = (bf16[192,1664]{1,0:T(8,128)(2,1)S(1)}, bf16[192,1664]{1,0:T(8,128)(2,1)S(1)}, u32[]{:S(2)}, u32[]{:S(2)}) collective-permute-start(bf16[192,1664]{1,0:T(8,128)(2,1)S(1)} %fusion.35), channel_id=1, source_target_pairs={{0,2},{1,3},{2,0},{3,1},{4,6},{5,7},{6,4},{7,5},{8,10},{9,11},{10,... | collective-permute-start | bytes 1916936 | tf_op jit(solution)/shard_map/ppermute | solution.py:331
  567.0 14.9 %collective-permute-start.46 = (bf16[24,6144]{1,0:T(8,128)(2,1)S(1)}, bf16[24,6144]{1,0:T(8,128)(2,1)S(1)}, u32[]{:S(2)}, u32[]{:S(2)}) collective-permute-start(bf16[24,6144]{1,0:T(8,128)(2,1)S(1)} %fusion.84), channel_id=1, source_target_pairs={{0,16},{4,20},{8,24},{12,28},{16,0},{20,4},{24,8},{28,12},{1,17},{... | collective-permute-start | bytes 884744 | tf_op jit(solution)/shard_map/ppermute | solution.py:331
  582.0 16.3 %collective-permute-start.47 = (bf16[48,6144]{1,0:T(8,128)(2,1)S(1)}, bf16[48,6144]{1,0:T(8,128)(2,1)S(1)}, u32[]{:S(2)}, u32[]{:S(2)}) collective-permute-start(bf16[48,6144]{1,0:T(8,128)(2,1)S(1)} %maximum_select_fusion.6), channel_id=1, source_target_pairs={{0,8},{4,12},{8,0},{12,4},{16,24},{20,28},{24,16},{28,20},{1,9},{5... | collective-permute-start | bytes 1769480 | tf_op jit(solution)/shard_map/ppermute | solution.py:331
  582.2 18.1 %collective-permute-start.20 = (bf16[48,1664]{1,0:T(8,128)(2,1)S(1)}, bf16[48,1664]{1,0:T(8,128)(2,1)S(1)}, u32[]{:S(2)}, u32[]{:S(2)}) collective-permute-start(bf16[48,1664]{1,0:T(8,128)(2,1)S(1)} %dynamic-slice_bitcast_fusion.7), channel_id=1, source_target_pairs={{0,8},{4,12},{8,0},{12,4},{16,24},{20,28},{24,16},{28,20},{1,9},{5... | collective-permute-start | bytes 479240 | tf_op jit(solution)/shard_map/ppermute | solution.py:331
  598.6 25.6 %collective-permute-start.48 = (bf16[96,6144]{1,0:T(8,128)(2,1)S(1)}, bf16[96,6144]{1,0:T(8,128)(2,1)S(1)}, u32[]{:S(2)}, u32[]{:S(2)}) collective-permute-start(bf16[96,6144]{1,0:T(8,128)(2,1)S(1)} %maximum_select_fusion.1), channel_id=1, source_target_pairs={{0,4},{4,0},{8,12},{12,8},{16,20},{20,16},{24,28},{28,24},{1,5},{5... | collective-permute-start | bytes 3538952 | tf_op jit(solution)/shard_map/ppermute | solution.py:331
  611.9 15.0 %collective-permute-start.23 = (bf16[48,1664]{1,0:T(8,128)(2,1)S(1)}, bf16[48,1664]{1,0:T(8,128)(2,1)S(1)}, u32[]{:S(2)}, u32[]{:S(2)}) collective-permute-start(bf16[48,1664]{1,0:T(8,128)(2,1)S(1)} %maximum_select_fusion.11), channel_id=1, source_target_pairs={{0,8},{4,12},{8,0},{12,4},{16,24},{20,28},{24,16},{28,20},{1,9},{5... | collective-permute-start | bytes 479240 | tf_op jit(solution)/shard_map/ppermute | solution.py:331
  (69 other events, 705.3 us)
Sparse Core Ops, SparseCore 0:
  46.4 100.5 all-gather.3
  149.7 58.7 all-gather.5
  252.7 73.2 reduce-scatter.4
  341.7 126.1 reduce-scatter.2

commit v3 on v1

--- a/solution.py
+++ b/solution.py
@@ -1,4 +1,5 @@
 import functools
+import math
 
 import jax
 import jax.numpy as jnp
@@ -144,19 +145,15 @@
             jax.ShapeDtypeStruct((heads, rows, LANES), jnp.float32),
         ],
         compiler_params=pltpu.CompilerParams(vmem_limit_bytes=VMEM_BYTES),
-        cost_estimate=pl.CostEstimate(
-            flops=8 * rows * key_total * width,
-            bytes_accessed=2 * heads * rows * key_total + 4 * key_total * width,
-            transcendentals=heads * rows * key_total,
-        ),
+        cost_estimate=pl.CostEstimate(flops=1, bytes_accessed=1, transcendentals=0),
         name="attention_forward",
     )(*(() if places is None else (places,)), *operands)
 
 
 def backward_kernel(head_size, biased, *refs):
     if biased:
-        (place_ref, q_ref, k_ref, v_ref, grad_ref, out_ref, weight_ref, inverse_ref,
-         dq_ref, dkv_ref, dist_ref, ds_ref, sum_ref) = refs
+        (q_ref, k_ref, v_ref, grad_ref, out_ref, weight_ref, inverse_ref,
+         dq_ref, dkv_ref, dist_ref, ds_ref) = refs
     else:
         (q_ref, k_ref, v_ref, grad_ref, out_ref, weight_ref, inverse_ref,
          dq_ref, dkv_ref, ds_ref) = refs
@@ -167,8 +164,6 @@
     dq = jnp.zeros(q_ref.shape, jnp.float32)
     grads = grad_ref[...].astype(jnp.float32)
     deltas = grads * out_ref[...].astype(jnp.float32)
-    if biased:
-        sum_ref[...] = jnp.zeros_like(sum_ref)
     scaled_all = []
     for head in range(group):
         inverse = inverse_ref[head]
@@ -187,9 +182,6 @@
                     ds_ref[head * rows + lo : head * rows + lo + piece, at : at + piece] = (
                         change.astype(jnp.bfloat16)
                     )
-                    if biased:
-                        place = place_ref[half * (key_total // piece) + at // piece]
-                        sum_ref[head, place] += change
         mixed = dot(ds_ref[head * rows : (head + 1) * rows, :], k_ref[...])
         dq = jnp.where(head_lanes(dq.shape, head, head_size), mixed, dq)
     dq_ref[...] = dq.astype(jnp.bfloat16)
@@ -208,77 +200,123 @@
             jnp.bfloat16
         )
     if biased:
-        steps = dist_ref.shape[1]
         down = lax.broadcasted_iota(jnp.int32, (piece, piece), 0)
         across = lax.broadcasted_iota(jnp.int32, (piece, piece), 1)
         flip = (down + across == piece - 1).astype(jnp.bfloat16)
-
-        def fold(step, carry):
-            for head in range(group):
-                block = sum_ref[head, step]
-                high = block.astype(jnp.bfloat16)
-                low = (block - high.astype(jnp.float32)).astype(jnp.bfloat16)
-                turned = dot(flip, high) + dot(flip, low)
-                padded = jnp.concatenate([turned, jnp.zeros_like(turned)], axis=1)
-                rolled = pltpu.roll(padded, piece + 1, 1, stride=1, stride_axis=0)
-                dist_ref[head, pl.ds(step, 1), :] = jnp.sum(rolled, axis=0, keepdims=True)
-            return carry
-
-        lax.fori_loop(0, steps, fold, 0)
+        for head in range(group):
+            for half in range(rows // piece):
+                lo = head * rows + half * piece
+                for start in range(0, key_total, wide):
+                    turned = dot(flip, ds_ref[lo : lo + piece, start : start + wide])
+                    for part in range(wide // piece):
+                        block = turned[:, part * piece : (part + 1) * piece]
+                        rolled = pltpu.roll(block, 1, 1, stride=1, stride_axis=0)
+                        later = jnp.sum(
+                            jnp.where(across <= down, rolled, 0.0), axis=0, keepdims=True
+                        )
+                        every = jnp.sum(rolled, axis=0, keepdims=True)
+                        at = half * (key_total // piece) + start // piece + part
+                        dist_ref[head, at : at + 1, :piece] = later
+                        dist_ref[head, at : at + 1, piece:] = every - later
 
 
 def attention_backward(
-    queries, key_values, grads, outs, weights, inverses, head_size, places=None, steps=0
+    queries, key_values, grads, outs, weights, inverses, head_size, biased, first=0, count=None
 ):
     rows, width = queries.shape
     key_total = key_values.shape[0]
     pairs = width // LANES
+    count = pairs if count is None else count
     group = LANES // head_size
-    heads = width // head_size
-    biased = places is not None
-    column = lambda shift: (lambda g, *_: (0, g + shift))
-    row_block = pl.BlockSpec((rows, LANES), column(0))
-    key_block = pl.BlockSpec((key_total, LANES), column(0))
-    out_specs = [row_block, pl.BlockSpec((2, key_total, LANES), lambda g, *_: (0, 0, g))]
+    column = lambda shift: (lambda g: (0, g + shift))
+    head_block = lambda g: (g + first, 0, 0)
+    row_block = pl.BlockSpec((rows, LANES), column(first))
+    blocks = rows // LANES * (key_total // LANES)
+    out_specs = [
+        pl.BlockSpec((rows, LANES), column(0)),
+        pl.BlockSpec((2, key_total, LANES), lambda g: (0, 0, g)),
+    ]
     out_shape = [
-        jax.ShapeDtypeStruct((rows, width), jnp.bfloat16),
-        jax.ShapeDtypeStruct((2, key_total, width), jnp.bfloat16),
+        jax.ShapeDtypeStruct((rows, count * LANES), jnp.bfloat16),
+        jax.ShapeDtypeStruct((2, key_total, count * LANES), jnp.bfloat16),
     ]
-    scratch = [pltpu.VMEM((group * rows, key_total), jnp.bfloat16)]
     if biased:
-        out_specs.append(pl.BlockSpec((group, steps, 2 * LANES), lambda g, *_: (g, 0, 0)))
-        out_shape.append(jax.ShapeDtypeStruct((heads, steps, 2 * LANES), jnp.float32))
-        scratch.append(pltpu.VMEM((group, steps + 1, LANES, LANES), jnp.float32))
-    grid_spec = pltpu.PrefetchScalarGridSpec(
-        num_scalar_prefetch=1 if biased else 0,
-        grid=(pairs,),
+        out_specs.append(pl.BlockSpec((group, blocks, 2 * LANES), lambda g: (g, 0, 0)))
+        out_shape.append(
+            jax.ShapeDtypeStruct((group * count, blocks, 2 * LANES), jnp.float32)
+        )
+    return pl.pallas_call(
+        functools.partial(backward_kernel, head_size, biased),
+        grid=(count,),
         in_specs=[
             row_block,
-            key_block,
-            pl.BlockSpec((key_total, LANES), column(pairs)),
+            pl.BlockSpec((key_total, LANES), column(first)),
+            pl.BlockSpec((key_total, LANES), column(first + pairs)),
             row_block,
             row_block,
-            pl.BlockSpec((group, rows, key_total), lambda g, *_: (g, 0, 0)),
-            pl.BlockSpec((group, rows, LANES), lambda g, *_: (g, 0, 0)),
+            pl.BlockSpec((group, rows, key_total), head_block),
+            pl.BlockSpec((group, rows, LANES), head_block),
         ],
         out_specs=out_specs,
-        scratch_shapes=scratch,
-    )
+        out_shape=out_shape,
+        scratch_shapes=[pltpu.VMEM((group * rows, key_total), jnp.bfloat16)],
+        compiler_params=pltpu.CompilerParams(vmem_limit_bytes=VMEM_BYTES),
+        cost_estimate=pl.CostEstimate(flops=1, bytes_accessed=1, transcendentals=0),
+        name="attention_backward",
+    )(queries, key_values, key_values, grads, outs, weights, inverses)
+
+
+def place_kernel(count, at_ref, *refs):
+    pieces, whole_ref, held_ref, in_sems, out_sems = refs[:count], *refs[count:]
+    rows = held_ref.shape[1]
+    parts = in_sems.shape[1]
+    width = held_ref.shape[2] // parts
+    loads, stores = [], []
+    for index in range(count):
+        start = pl.multiple_of(at_ref[index] * rows, rows)
+        for part in range(parts):
+            columns = pl.ds(part * width, width)
+            held = held_ref.at[index, :, columns]
+            loads.append(
+                pltpu.make_async_copy(
+                    pieces[index].at[:, columns], held, in_sems.at[index, part]
+                )
+            )
+            stores.append(
+                pltpu.make_async_copy(
+                    held, whole_ref.at[pl.ds(start, rows), columns], out_sems.at[index, part]
+                )
+            )
+    for load in loads:
+        load.start()
+    for load, store in zip(loads, stores):
+        load.wait()
+        store.start()
+    for store in stores:
+        store.wait()
+
+
+def place_rows(pieces, places):
+    rows, width = pieces[0].shape
+    count = len(pieces)
+    parts = width // 1024
     return pl.pallas_call(
-        functools.partial(backward_kernel, head_size, biased),
-        grid_spec=grid_spec,
-        out_shape=out_shape,
+        functools.partial(place_kernel, count),
+        grid_spec=pltpu.PrefetchScalarGridSpec(
+            num_scalar_prefetch=1,
+            grid=(1,),
+            in_specs=[pl.BlockSpec(memory_space=pl.ANY)] * count,
+            out_specs=pl.BlockSpec(memory_space=pl.ANY),
+            scratch_shapes=[
+                pltpu.VMEM((count, rows, width), pieces[0].dtype),
+                pltpu.SemaphoreType.DMA((count, parts)),
+                pltpu.SemaphoreType.DMA((count, parts)),
+            ],
+        ),
+        out_shape=jax.ShapeDtypeStruct((rows * count, width), pieces[0].dtype),
         compiler_params=pltpu.CompilerParams(vmem_limit_bytes=VMEM_BYTES),
-        cost_estimate=pl.CostEstimate(
-            flops=16 * rows * key_total * width,
-            bytes_accessed=2 * heads * rows * key_total + 8 * key_total * width,
-            transcendentals=0,
-        ),
-        name="attention_backward",
-    )(
-        *((places,) if biased else ()),
-        queries, key_values, key_values, grads, outs, weights, inverses,
-    )
+        name="place_rows",
+    )(jnp.stack(places).astype(jnp.int32), *pieces)
 
 
 EPSILON = 1e-06
@@ -321,9 +359,171 @@
     return pieces[:, :, ::-1].reshape(heads, -1)[:, block - 1 : block - 1 + steps * block]
 
 
-def reduce_weight(grad):
-    share = lax.psum_scatter(rounded(grad), ("fsdp", "ctx"), scatter_dimension=0, tiled=True)
-    return lax.all_gather(share, "ctx", axis=0, tiled=True).astype(jnp.float32)
+def bit_count(axis_name):
+    return int(math.log2(lax.axis_size(axis_name)))
+
+
+def swap(values, axis_name, bit):
+    size = lax.axis_size(axis_name)
+    return lax.ppermute(values, axis_name, [(i, i ^ (1 << bit)) for i in range(size)])
+
+
+def own_bit(axis_name, bit):
+    return (lax.axis_index(axis_name) >> bit) & 1
+
+
+def pick(values, index, axis):
+    return lax.dynamic_index_in_dim(values, index, axis, keepdims=False)
+
+
+def after(value, *others):
+    return lax.optimization_barrier((value,) + others)[0]
+
+
+def far_rows(share):
+    held = [(share, lax.axis_index("fsdp"))]
+    for bit in reversed(range(1, bit_count("fsdp"))):
+        held = held + [(swap(piece, "fsdp", bit), at ^ (1 << bit)) for piece, at in held]
+    return held
+
+
+def near_rows(held):
+    return held + [(swap(piece, "fsdp", 0), at ^ 1) for piece, at in held]
+
+
+def whole_rows(held):
+    held = near_rows(held)
+    return place_rows([piece for piece, _ in held], [at for _, at in held])
+
+
+class Product:
+    def __init__(self, left, right, parts):
+        bits = int(math.log2(parts))
+        self.left = left.reshape((left.shape[0],) + (2,) * bits + (left.shape[1] // parts,))
+        self.right = right
+
+    def take(self, bit):
+        part = Product.__new__(Product)
+        part.left = pick(self.left, bit, self.left.ndim - 2)
+        part.right = self.right
+        return part
+
+    def value(self):
+        return t_dot(self.left, self.right)
+
+
+class Ready:
+    def __init__(self, values, parts):
+        bits = int(math.log2(parts))
+        self.values = values.reshape(
+            (2,) * bits + (values.shape[0] // parts, values.shape[1])
+        )
+
+    def take(self, bit):
+        part = Ready.__new__(Ready)
+        part.values = pick(self.values, bit, self.values.ndim - 3)
+        return part
+
+    def value(self):
+        return self.values
+
+
+def joined(own, other, mine):
+    return jnp.where(
+        mine == 0, jnp.stack([own, other], axis=-3), jnp.stack([other, own], axis=-3)
+    )
+
+
+class Reduction:
+    def __init__(self, terms, *stages):
+        self.terms = terms
+        self.received = []
+        self.kept = None
+        self.pending = None
+        self.gathered = None
+        self.plan = []
+        for stage in stages:
+            bits = [(stage, bit) for bit in range(bit_count("fsdp" if stage == "fsdp" else "ctx"))]
+            self.plan += reversed(bits) if stage == "gather" else bits
+
+    def shard(self):
+        total = jnp.concatenate([term.value() for term in self.terms], axis=-1)
+        for item in self.received:
+            total = total + item.astype(jnp.float32)
+        return rounded(total)
+
+    def merged(self):
+        if self.gathered is not None:
+            own, bit = self.gathered
+            return joined(own, self.pending, own_bit("ctx", bit))
+        if self.kept is not None:
+            return rounded(self.kept.astype(jnp.float32) + self.pending.astype(jnp.float32))
+        total = self.shard()
+        parts = lax.axis_size("ctx")
+        return total.reshape(
+            (2,) * bit_count("ctx") + (total.shape[0] // parts, total.shape[1])
+        )
+
+    def settle(self, main):
+        main = tuple(main)
+        if self.pending is not None:
+            self.pending, *main = lax.optimization_barrier((self.pending,) + main)
+        elif self.received:
+            *self.received, last = lax.optimization_barrier(tuple(self.received) + (main,))
+            main = last
+        return tuple(main)
+
+    def prepare(self):
+        kind, bit = self.step = self.plan.pop(0)
+        if kind == "gather":
+            total = self.merged()
+            self.gathered = (total, bit)
+            return total
+        mine = own_bit(kind, bit)
+        if kind == "ctx":
+            total = self.merged()
+            self.kept = pick(total, mine, total.ndim - 3)
+            return pick(total, 1 - mine, total.ndim - 3)
+        send = jnp.concatenate([term.take(1 - mine).value() for term in self.terms], axis=-1)
+        for item in self.received:
+            send = send + pick(item, 1 - mine, item.ndim - 3).astype(jnp.float32)
+        self.terms = [term.take(mine) for term in self.terms]
+        self.received = [pick(item, mine, item.ndim - 3) for item in self.received]
+        return rounded(send)
+
+    def exchange(self, send):
+        kind, bit = self.step
+        other = swap(send, "fsdp" if kind == "fsdp" else "ctx", bit)
+        if kind == "fsdp":
+            self.received.append(other)
+        else:
+            self.pending = other
+
+    def result(self):
+        total = self.merged()
+        return total.reshape(-1, total.shape[-1])
+
+
+def finish(item):
+    while item.plan:
+        advance([item])
+    return item.shard()
+
+
+def advance(sums, *main):
+    if main:
+        for item in sums:
+            main = item.settle(main)
+    sends = [item.prepare() for item in sums]
+    held = lax.optimization_barrier(tuple(sends) + tuple(main))
+    for item, send in zip(sums, held):
+        item.exchange(send)
+    main = held[len(sums) :]
+    return main[0] if len(main) == 1 else main
+
+
+def weighed(weight, grad):
+    return jnp.sum(weight.astype(jnp.float32) * grad[:, : weight.shape[1]], axis=1)
 
 
 def body(tokens, encoded, cotangent, w_self, w_cross, w_ffn, gains, table, bucket_ids, block_order):
@@ -336,11 +536,26 @@
     seq_length = bucket_ids.shape[0]
     steps = seq_length // block
     ctx_place = lax.axis_index("ctx")
-    table_rows = lax.all_gather(table, "fsdp", axis=0, tiled=True)
-    gain_rows = lax.all_gather(gains, "fsdp", axis=1, tiled=True)
-    whole_self = lax.all_gather(w_self, "fsdp", axis=0, tiled=True)
-    whole_cross = lax.all_gather(w_cross, "fsdp", axis=0, tiled=True)
-    whole_ffn = lax.all_gather(w_ffn, "fsdp", axis=0, tiled=True)
+    fsdp_size = lax.axis_size("fsdp")
+    small = jnp.concatenate([gains.reshape(1, -1), table.reshape(1, -1)], axis=1)
+    far_small = far_rows(small)
+    held_self = far_rows(w_self)
+    held_self = near_rows(
+        [(after(piece, *[other for other, _ in far_small[1:]]), at) for piece, at in held_self]
+    )
+    small_held = near_rows(far_small)
+    small = jnp.zeros((fsdp_size, small.shape[1]), small.dtype)
+    for piece, at in small_held:
+        small = lax.dynamic_update_slice_in_dim(small, piece, at, 0)
+    gain_rows = jnp.transpose(
+        small[:, : gains.size].reshape((fsdp_size,) + gains.shape), (1, 0, 2)
+    ).reshape(gains.shape[0], -1)
+    table_rows = small[:, gains.size :].reshape(-1, head_count)
+    row_pair = jnp.concatenate([tokens[0], encoded[0]], axis=0)
+    row_pairs = lax.all_gather(row_pair, "ctx", axis=0, tiled=False)
+    held_cross = far_rows(after(w_cross, small, *[piece for piece, _ in held_self[1:]]))
+    held_ffn = far_rows(after(w_ffn, *[piece for piece, _ in held_cross[1:]]))
+    whole_self = place_rows([piece for piece, _ in held_self], [at for _, at in held_self])
     gain_float = gain_rows.astype(jnp.float32)
     bucket_count = table_rows.shape[0]
     in_bucket = (
@@ -352,26 +567,35 @@
         (((0,), (0,)), ((), ())),
         precision=lax.Precision.HIGHEST,
     )
-    tiles = bias_tiles(distance_rows(by_distance, block), LANES // head_size)
+    tiles = bias_tiles(
+        after(distance_rows(by_distance, block), whole_self), LANES // head_size
+    )
     own_blocks = lax.dynamic_slice_in_dim(block_order, 2 * ctx_place, 2)
     apart = own_blocks[:, None] - block_order[None, :]
     places = jnp.where(apart < 0, steps, apart).astype(jnp.int32).reshape(-1)
 
     inputs = tokens[0].astype(jnp.float32)
-    encoder_rows = encoded[0]
+    held_cross = near_rows([(after(piece, tiles), at) for piece, at in held_cross])
+    whole_cross = place_rows([piece for piece, _ in held_cross], [at for _, at in held_cross])
+    row_pairs = after(row_pairs, whole_cross)
+    encoder_all = row_pairs[:, row_count:].reshape(-1, model_width)
+    normed_all = rounded(
+        row_norm(row_pairs[:, :row_count].astype(jnp.float32), gain_float[0])
+    ).reshape(-1, model_width)
     normed_one = rounded(row_norm(inputs, gain_float[0]))
-    projected = rounded(dot(normed_one, whole_self[:, : 3 * model_width]))
-    queries = projected[:, :model_width]
-    key_values = lax.all_gather(projected[:, model_width:], "ctx", axis=0, tiled=True)
-    encoder_local = rounded(dot(encoder_rows, whole_cross[:, model_width : 3 * model_width]))
-    encoder_kv = lax.all_gather(encoder_local, "ctx", axis=0, tiled=True)
+    queries = rounded(dot(normed_one, whole_self[:, :model_width]))
+    key_values = rounded(dot(normed_all, whole_self[:, model_width : 3 * model_width]))
     attended, weights, inverses = attention_forward(queries, key_values, head_size, tiles, places)
+    held_ffn = near_rows([(after(piece, attended), at) for piece, at in held_ffn])
+    encoder_kv = rounded(dot(encoder_all, whole_cross[:, model_width : 3 * model_width]))
     after_one = inputs + dot(attended, whole_self[:, 3 * model_width :])
     normed_two = rounded(row_norm(after_one, gain_float[1]))
     cross_query = rounded(dot(normed_two, whole_cross[:, :model_width]))
     cross_rows, cross_weights, cross_inverses = attention_forward(
         cross_query, encoder_kv, head_size
     )
+    held_ffn = [(after(piece, cross_rows), at) for piece, at in held_ffn]
+    whole_ffn = place_rows([piece for piece, _ in held_ffn], [at for _, at in held_ffn])
     after_two = after_one + dot(cross_rows, whole_cross[:, 3 * model_width :])
     normed_three = rounded(row_norm(after_two, gain_float[2]))
     gate_up = dot(normed_three, whole_ffn[:, : 2 * hidden_units])
@@ -384,47 +608,73 @@
     grad_mixed = dot(grad_branch_three, whole_ffn[:, 2 * hidden_units :])
     grad_gate_up = rounded(gated_back(grad_mixed)[0])
     grad_normed_three = dot_t(grad_gate_up, whole_ffn[:, : 2 * hidden_units])
-    ffn_grad = reduce_weight(
-        jnp.concatenate(
-            [
-                rounded(t_dot(normed_three, grad_gate_up)),
-                rounded(t_dot(grad_branch_three, mixed_rows)),
-            ],
-            axis=1,
-        )
-    )
-    norm_part, gain_three = jax.vjp(row_norm, after_two, gain_float[2])[1](grad_normed_three)
+    ffn_sum = Reduction(
+        [
+            Product(normed_three, grad_gate_up, fsdp_size),
+            Product(grad_branch_three, mixed_rows, fsdp_size),
+        ],
+        "fsdp",
+    )
+    grad_normed_three = advance([ffn_sum], grad_normed_three)
+    norm_part = jax.vjp(row_norm, after_two, gain_float[2])[1](grad_normed_three)[0]
     grad_after_one = grad_after_two + norm_part
     grad_branch_two = rounded(grad_after_one)
     grad_cross_rows = rounded(dot_t(grad_branch_two, whole_cross[:, 3 * model_width :]))
+    grad_cross_rows = advance([ffn_sum], grad_cross_rows)
     grad_cross_query, encoder_full = attention_backward(
         cross_query, encoder_kv, grad_cross_rows, cross_rows, cross_weights, cross_inverses,
-        head_size,
-    )
-    encoder_own = lax.psum_scatter(encoder_full, "ctx", scatter_dimension=1, tiled=True)
+        head_size, False,
+    )
     grad_normed_two = dot_t(grad_cross_query, whole_cross[:, :model_width])
-    norm_part, gain_two = jax.vjp(row_norm, after_one, gain_float[1])[1](grad_normed_two)
+    norm_part = jax.vjp(row_norm, after_one, gain_float[1])[1](grad_normed_two)[0]
     grad_inputs_one = grad_after_one + norm_part
     grad_branch_one = rounded(grad_inputs_one)
     grad_attended = rounded(dot_t(grad_branch_one, whole_self[:, 3 * model_width :]))
-    grad_query, grad_key_full, distance_sums = attention_backward(
-        queries, key_values, grad_attended, attended, weights, inverses, head_size, places, steps
-    )
-    grad_key_own = lax.psum_scatter(grad_key_full, "ctx", scatter_dimension=1, tiled=True)
-
-    grad_encoder_kv = jnp.concatenate([encoder_own[0], encoder_own[1]], axis=1)
-    grad_encoded = rounded(
-        dot_t(grad_encoder_kv, whole_cross[:, model_width : 3 * model_width])
-    )
-    cross_grad = reduce_weight(
-        jnp.concatenate(
-            [
-                rounded(t_dot(normed_two, grad_cross_query)),
-                rounded(t_dot(encoder_rows, grad_encoder_kv)),
-                rounded(t_dot(cross_rows, grad_branch_two)),
-            ],
-            axis=1,
-        )
+    cross_sum = Reduction(
+        [
+            Product(normed_two, grad_cross_query, fsdp_size),
+            Product(encoder_all, encoder_full[0], fsdp_size),
+            Product(encoder_all, encoder_full[1], fsdp_size),
+            Product(cross_rows, grad_branch_two, fsdp_size),
+        ],
+        "fsdp",
+    )
+    grad_encoder_part = rounded(
+        dot_t(encoder_full[0], whole_cross[:, model_width : 2 * model_width])
+        + dot_t(encoder_full[1], whole_cross[:, 2 * model_width : 3 * model_width])
+    )
+    encoder_sum = Reduction([Ready(grad_encoder_part, 1)], "ctx")
+    grad_attended = advance([cross_sum, encoder_sum], grad_attended)
+    grad_query, grad_keys, distance_sums = attention_backward(
+        queries, key_values, grad_attended, attended, weights, inverses, head_size, True
+    )
+    ffn_shard, grad_query, grad_keys, distance_sums = lax.optimization_barrier(
+        (finish(ffn_sum), grad_query, grad_keys, distance_sums)
+    )
+    grad_query, grad_keys = advance([cross_sum], grad_query, grad_keys)
+    ffn_shard = lax.psum_scatter(ffn_shard, "ctx", scatter_dimension=0, tiled=True)
+    self_sum = Reduction(
+        [
+            Product(normed_one, grad_query, fsdp_size),
+            Product(normed_all, grad_keys[0], fsdp_size),
+            Product(normed_all, grad_keys[1], fsdp_size),
+            Product(attended, grad_branch_one, fsdp_size),
+        ],
+        "fsdp",
+    )
+    grad_keys = advance([self_sum], grad_keys)
+    key_weights = whole_self[:, model_width : 2 * model_width]
+    value_weights = whole_self[:, 2 * model_width : 3 * model_width]
+    grad_normed_part = rounded(
+        dot_t(grad_keys[0], key_weights) + dot_t(grad_keys[1], value_weights)
+    )
+    token_sum = Reduction([Ready(grad_normed_part, 1)], "ctx")
+    distance_sums = advance([token_sum, encoder_sum], distance_sums)
+    cross_shard, distance_sums = lax.optimization_barrier((finish(cross_sum), distance_sums))
+    distance_sums = advance([self_sum], distance_sums)
+    in_place = (places[None, :] == jnp.arange(steps, dtype=jnp.int32)[:, None]).astype(jnp.float32)
+    distance_sums = jnp.einsum(
+        "sp,hpw->hsw", in_place, distance_sums, precision=lax.Precision.HIGHEST
     )
     grad_table = lax.dot_general(
         in_bucket,
@@ -432,31 +682,37 @@
         (((1,), (1,)), ((), ())),
         precision=lax.Precision.HIGHEST,
     )
-    grad_projected = jnp.concatenate([grad_query, grad_key_own[0], grad_key_own[1]], axis=1)
-    grad_normed_one = dot_t(grad_projected, whole_self[:, : 3 * model_width])
-    self_grad = reduce_weight(
-        jnp.concatenate(
-            [
-                rounded(t_dot(normed_one, grad_projected)),
-                rounded(t_dot(attended, grad_branch_one)),
-            ],
-            axis=1,
-        )
-    )
-    norm_part, gain_one = jax.vjp(row_norm, inputs, gain_float[0])[1](grad_normed_one)
+    grad_normed_query = dot_t(grad_query, whole_self[:, :model_width])
+    for bit in range(bit_count("fsdp")):
+        grad_table = grad_table + swap(grad_table, "fsdp", bit)
+    table_columns = jnp.pad(
+        lax.dynamic_slice_in_dim(
+            grad_table, lax.axis_index("fsdp") * table.shape[0], table.shape[0], 0
+        ),
+        ((0, gains.shape[1] - table.shape[0]), (0, LANES - head_count)),
+    )
+    rest = jnp.concatenate([cross_shard, finish(self_sum), rounded(table_columns)], axis=1)
+    rest_sum = Reduction([Ready(rest, 1)], "ctx", "gather")
+    sums = [rest_sum, token_sum, encoder_sum]
+    while any(item.plan for item in sums):
+        advance([item for item in sums if item.plan])
+    ffn_rows = lax.all_gather(ffn_shard, "ctx", axis=0, tiled=True)
+    grad_normed_one = grad_normed_query + token_sum.result().astype(jnp.float32)
+    norm_part = jax.vjp(row_norm, inputs, gain_float[0])[1](grad_normed_one)[0]
     grad_tokens = rounded(grad_inputs_one + norm_part)
-    gain_terms = jnp.stack([gain_one, gain_two, gain_three])
-    small = jnp.concatenate([gain_terms.reshape(-1), grad_table.reshape(-1)])
-    small = lax.psum(small, ("fsdp", "ctx"))
-    fsdp_place = lax.axis_index("fsdp")
-    gain_total = small[: gain_terms.size].reshape(gain_terms.shape)
-    table_total = small[gain_terms.size :].reshape(grad_table.shape)
-    gain_own = lax.dynamic_slice_in_dim(
-        gain_total, fsdp_place * gains.shape[1], gains.shape[1], axis=1
-    )
-    table_own = lax.dynamic_slice_in_dim(
-        table_total, fsdp_place * table.shape[0], table.shape[0], axis=0
-    )
+    grad_encoded = encoder_sum.result()
+    ffn_grad = ffn_rows.astype(jnp.float32)
+    rest = rest_sum.result().astype(jnp.float32)
+    cross_grad = rest[:, : 4 * model_width]
+    self_grad = rest[:, 4 * model_width : 8 * model_width]
+    table_own = rest[: table.shape[0], 8 * model_width : 8 * model_width + head_count]
+    gain_own = jnp.stack(
+        [
+            weighed(w_self[:, : 3 * model_width], self_grad),
+            weighed(w_cross[:, :model_width], cross_grad),
+            weighed(w_ffn[:, : 2 * hidden_units], ffn_grad),
+        ]
+    ) / gains.astype(jnp.float32)
     return (
         output[None],
         grad_tokens[None],

time: 1050 us -> 576 us (0.55); the launches traced: 1050 us -> 565 us
  waiting for transfers between devices: 789 us -> 223 us
  blocking collectives: 51.8 us -> 0 us
  matrix products: 55.6 us -> 96.2 us
  other arithmetic: 22.8 us -> 61.5 us
  local copies, waits for them, and re-layouts: 18.6 us -> 51 us
  starting transfers between devices: 1 us -> 25.9 us
    reduce_scatter x5 -> x1, waiting for transfers between devices: 468 us -> 0.01 us  [body(): lax.psum_scatter(ffn_shard, 'ctx', scatter_dimension=0, tiled=True)]
    all_gather x8 -> x2, waiting for transfers between devices: 319 us -> 11 us  [the longest x1 11 us: body(): row_pairs = lax.all_gather(row_pair, 'ctx', axis=0, tiled=False)]
    ppermute x0 -> x32, waiting for transfers between devices: none -> 212 us  [swap(): lax.ppermute(values, axis_name, [(i, i ^ 1 << bit) for i in range(size)])]
    psum x1 -> x0, blocking collectives: 40.6 us -> none  [body(): small = lax.psum(small, ('fsdp', 'ctx'))]
    dot_general x7 -> x30, matrix products: 13 us -> 41.3 us  [t_dot(): lax.dot_general(left, right, (((0,), (0,)), ((), ())), preferred_element_...]
    convert_element_type x3 -> x22, other arithmetic: 10.3 us -> 37.8 us  [the longest x20 35.1 us: rounded(): return values.astype(jnp.bfloat16)]
    ppermute x0 -> x32, starting transfers between devices: none -> 25.6 us  [swap(): lax.ppermute(values, axis_name, [(i, i ^ 1 << bit) for i in range(size)])]
    pallas_call x2, Pallas kernels: 60.5 us -> 37.5 us  [attention_backward(): pl.pallas_call(functools.partial(backward_kernel, head_size, biased), gri...]
  transfers between devices with their start and end apart: 13 -> 35, of which waited for: 12 -> 18; matrix products, arithmetic and copies ran while one was open for 7% -> 29% of each run, Pallas kernels for 8% -> 13%
where the time goes in v3:
time: 576 us; the launch traced here: 565 us
  waiting for transfers between devices  223 us (39%)
  matrix products  96.2 us (17%)
  Pallas kernels  91.9 us (16%)
  other arithmetic  61.5 us (11%)
  local copies, waits for them, and re-layouts  51 us (9%)
  starting transfers between devices  25.9 us (4%)
  between operations  15.4 us (3%)
    ppermute x32, waiting for transfers between devices, swap(): lax.ppermute(values, axis_name, [(i, i ^ 1 << bit) for i in range(size)])  212 us
    dot_general x30, matrix products, t_dot(): lax.dot_general(left, right, (((0,), (0,)), ((), ())), preferred_element_...  41.3 us
    pallas_call x2, Pallas kernels, attention_backward(): pl.pallas_call(functools.partial(backward_kernel, head_size, biased), gri...  37.5 us
    convert_element_type x20, other arithmetic, rounded(): return values.astype(jnp.bfloat16)  35.1 us
    dot_general x8, matrix products, dot(): lax.dot_general(left, right, (((1,), (0,)), ((), ())), preferred_element_...  29.8 us
    pallas_call x2, Pallas kernels, attention_forward(): pl.pallas_call(functools.partial(forward_kernel, head_size, tiles is not...  29.2 us
    ppermute x32, starting transfers between devices, swap(): lax.ppermute(values, axis_name, [(i, i ^ 1 << bit) for i in range(size)])  25.6 us
    dot_general x10, matrix products, dot_t(): lax.dot_general(left, right, (((1,), (1,)), ((), ())), preferred_element_...  24.4 us
  transfers between devices with their start and end apart: 35, of which 18 were waited for; matrix products, arithmetic and copies ran while one was open for 29% of the time, Pallas kernels for 13%

profile of v3, /device:TPU:0, one launch (start us, length us, event | category | flops | bytes accessed | tf_op | source)
XLA Modules:
  0.0 564.9 jit_solution(17318513710353972946)
XLA Ops:
  13.9 24.6 %collective-permute-done = bf16[1,672]{1,0:T(2,128)(2,1)S(1)} collective-permute-done((bf16[1,672]{1,0:T(2,128)(2,1)S(1)}, bf16[1,672]{1,0:T(2,128)(2,1)S(1)}, u32[]{:S(2)}, u32[]{:S(2)}) %collective-permute-start) | collective-permute-done | bytes 1376 | tf_op jit(solution)/shard_map/ppermute | solution.py:368
  50.5 5.0 place_rows.3
  55.5 6.7 %bias_tiles.1.refs_4_ = bf16[12,17,128,128]{3,2,1,0:T(8,128)(2,1)} custom-call(f32[12,17,256]{2,1,0:T(8,128)} %select_maximum_fusion.vector_ref), custom_call_target="tpu_custom_call" | custom-call | tf_op jit(solution)/shard_map/bias_tiles/pallas_call | solution.py:57
  62.2 9.2 %collective-permute-done.6.refs_1_ = bf16[192,3072]{1,0:T(8,128)(2,1)} collective-permute-done((bf16[192,3072]{1,0:T(8,128)(2,1)}, bf16[192,3072]{1,0:T(8,128)(2,1)}, u32[]{:S(2)}, u32[]{:S(2)}) %collective-permute-start.6) | collective-permute-done | bytes 1179680 | tf_op jit(solution)/shard_map/ppermute | solution.py:368
  76.8 5.1 place_rows.4
  81.9 11.0 %all-gather.6.cloned.1.call-done = bf16[3072,768]{1,0:T(8,128)(2,1)} async-done(((bf16[384,768]{1,0:T(8,128)(2,1)}), bf16[3072,768]{1,0:T(8,128)(2,1)}) %all-gather.6.cloned.1.call-update) | async-done | bytes 4718608 | tf_op jit(solution)/shard_map/all_gather | solution.py:555
  92.8 7.0 %copy.32 = bf16[8,384,768]{1,0,2:T(8,128)(2,1)} copy(bf16[8,384,768]{2,1,0:T(8,128)(2,1)} %bitcast.348) | data formatting | bytes 9437184 | tf_op jit(solution)/shard_map/optimization_barrier | solution.py:380
  102.8 3.6 fusion.2
  108.1 7.3 %convolution_convert_fusion.refs_2_.refs_3_.refs_1_ = bf16[2048,1536]{1,0:T(8,128)(2,1)} fusion(bf16[2048,768]{0,1:T(8,128)(2,1)S(1)} %bitcast.349, bf16[768,3072]{1,0:T(8,128)(2,1)S(1)} %bitcast.345), kind=kOutput, calls=%fused_computation.2 | convolution fusion | flops 4834983936 | bytes 11796480 | tf_op jit(solution)/shard_map/dot_general | solution.py:17
  115.5 18.6 %attention_forward.2 = (bf16[256,768]{1,0:T(8,128)(2,1)}, bf16[12,256,2048]{2,1,0:T(8,128)(2,1)}, f32[12,256,128]{2,1,0:T(8,128)}) custom-call(s32[32]{0:T(128)} %compare_select_fusion.refs_0_, bf16[256,768]{1,0:T(8,128)(2,1)} %convolution_convert_fusion.11.refs_1_.refs_0_, bf16[2048,1536]{1,0:T(8,128)(2,1)} %convolution_convert_fusion.refs_2_.refs_3_.refs_1_, ...), custom_call_target="tpu_custom_call" | custom-call | flops 1 | bytes 1 | tf_op jit(solution)/shard_map/attention_forward/pallas_call | solution.py:139
  141.1 5.9 %convolution_convert_fusion.2.refs_1_.refs_2_ = bf16[1024,1536]{1,0:T(8,128)(2,1)} fusion(bf16[768,3072]{1,0:T(8,128)(2,1)} %place_rows.4, bf16[96,8,8,128]{3,2,1,0:T(8,128)(2,1)S(1)} %bitcast.339), kind=kOutput, calls=%fused_computation.21 | convolution fusion | flops 2417491968 | bytes 7077888 | tf_op jit(solution)/shard_map/dot_general | solution.py:17
  147.1 10.6 %attention_forward.3 = (bf16[256,768]{1,0:T(8,128)(2,1)}, bf16[12,256,1024]{2,1,0:T(8,128)(2,1)}, f32[12,256,128]{2,1,0:T(8,128)}) custom-call(bf16[256,768]{1,0:T(8,128)(2,1)} %convolution_convert_fusion.10.refs_0_, bf16[1024,1536]{1,0:T(8,128)(2,1)} %convolution_convert_fusion.2.refs_1_.refs_2_, bf16[1024,1536]{1,0:T(8,128)(2,1)} %convolution_convert_fusion.2.refs_1_.refs_2_), custom_call_target="tpu_custom_call" | custom-call | flops 1 | bytes 1 | tf_op jit(solution)/shard_map/attention_forward/pallas_call | solution.py:139
  160.7 8.3 %place_rows.5 = bf16[768,6144]{1,0:T(8,128)(2,1)} custom-call(s32[4]{0:T(128)} %pad_add_fusion.1.at_ref, bf16[192,6144]{1,0:T(8,128)(2,1)} %refs_0_.2, bf16[192,6144]{1,0:T(8,128)(2,1)} %collective-permute-done.9.refs_1_, bf16[192,6144]{1,0:T(8,128)(2,1)} %collective-permute-done.10.refs_2_, bf16[192,6144]{1,0:T(8,128)(2,1)} %collective-permute-done.11.refs_3_), custom_call_target="tpu_custom_call" | custom-call | tf_op jit(solution)/shard_map/place_rows/pallas_call | solution.py:303
  169.1 4.7 fusion.5
  187.3 3.7 reshape_reshape.8
  190.9 6.3 %reshape_reshape.9 = bf16[2048,2,2,192]{0,3,2,1:T(8,128)(2,1)} reshape(bf16[8,256,768]{1,0,2:T(8,128)(2,1)} %copy-done) | data formatting | bytes 6291456 | tf_op jit(solution)/shard_map/reshape;reshape | solution.py:402
  214.8 3.6 fusion.8
  218.4 11.7 %attention_backward.2 = (bf16[256,768]{1,0:T(8,128)(2,1)}, bf16[2,1024,768]{2,1,0:T(8,128)(2,1)}) custom-call(bf16[256,768]{1,0:T(8,128)(2,1)} %convolution_convert_fusion.10.refs_0_, bf16[1024,1536]{1,0:T(8,128)(2,1)} %convolution_convert_fusion.2.refs_1_.refs_2_, bf16[1024,1536]{1,0:T(8,128)(2,1)} %convolution_convert_fusion.2.refs_1_.refs_2_, ...), custom_call_target="tpu_custom_call" | custom-call | flops 1 | bytes 1 | tf_op jit(solution)/shard_map/attention_backward/pallas_call | solution.py:248
  254.1 25.8 %attention_backward.3 = (bf16[256,768]{1,0:T(8,128)(2,1)}, bf16[2,2048,768]{2,1,0:T(8,128)(2,1)}, f32[12,32,256]{2,1,0:T(8,128)}) custom-call(bf16[256,768]{1,0:T(8,128)(2,1)} %convolution_convert_fusion.11.refs_1_.refs_0_, bf16[2048,1536]{1,0:T(8,128)(2,1)} %convolution_convert_fusion.refs_2_.refs_3_.refs_1_, ...), custom_call_target="tpu_custom_call" | custom-call | flops 1 | bytes 1 | tf_op jit(solution)/shard_map/attention_backward/pallas_call | solution.py:248
  286.9 8.6 %collective-permute-done.14 = bf16[192,6144]{1,0:T(8,128)(2,1)} collective-permute-done((bf16[192,6144]{1,0:T(8,128)(2,1)}, bf16[192,6144]{1,0:T(8,128)(2,1)}, u32[]{:S(2)}, u32[]{:S(2)}) %collective-permute-start.14) | collective-permute-done | bytes 2359328 | tf_op jit(solution)/shard_map/ppermute | solution.py:368
  295.5 4.8 fusion.10
  303.4 3.7 fusion.24
  307.1 3.5 fusion.18
  339.6 3.8 collective-permute-done.17
  353.9 24.9 %collective-permute-done.16 = bf16[2,2,256,768]{3,2,0,1:T(8,128)(2,1)} collective-permute-done((bf16[2,2,256,768]{3,2,0,1:T(8,128)(2,1)}, bf16[2,2,256,768]{3,2,0,1:T(8,128)(2,1)}, u32[]{:S(2)}, u32[]{:S(2)}) %collective-permute-start.16) | collective-permute-done | bytes 1572896 | tf_op jit(solution)/shard_map/ppermute | solution.py:368
  391.9 27.6 %collective-permute-done.23 = bf16[2,256,768]{2,1,0:T(8,128)(2,1)} collective-permute-done((bf16[2,256,768]{2,1,0:T(8,128)(2,1)}, bf16[2,256,768]{2,1,0:T(8,128)(2,1)}, u32[]{:S(2)}, u32[]{:S(2)}) %collective-permute-start.23) | collective-permute-done | bytes 786464 | tf_op jit(solution)/shard_map/ppermute | solution.py:368
  424.9 3.9 fusion.109
  432.4 18.6 %collective-permute-done.27 = bf16[2,24,6272]{2,1,0:T(8,128)(2,1)} collective-permute-done((bf16[2,24,6272]{2,1,0:T(8,128)(2,1)S(1)}, bf16[2,24,6272]{2,1,0:T(8,128)(2,1)}, u32[]{:S(2)}, u32[]{:S(2)}) %collective-permute-start.27) | collective-permute-done | bytes 602144 | tf_op jit(solution)/shard_map/ppermute | solution.py:368
  454.8 16.2 %collective-permute-done.28 = bf16[24,6272]{1,0:T(8,128)(2,1)S(1)} collective-permute-done((bf16[24,6272]{1,0:T(8,128)(2,1)S(1)}, bf16[24,6272]{1,0:T(8,128)(2,1)S(1)}, u32[]{:S(2)}, u32[]{:S(2)}) %collective-permute-start.28) | collective-permute-done | bytes 301088 | tf_op jit(solution)/shard_map/ppermute | solution.py:368
  472.2 27.7 %collective-permute-done.29 = bf16[24,6272]{1,0:T(8,128)(2,1)S(1)} collective-permute-done((bf16[24,6272]{1,0:T(8,128)(2,1)S(1)}, bf16[24,6272]{1,0:T(8,128)(2,1)S(1)}, u32[]{:S(2)}, u32[]{:S(2)}) %collective-permute-start.29) | collective-permute-done | bytes 301088 | tf_op jit(solution)/shard_map/ppermute | solution.py:368
  501.4 15.2 %collective-permute-done.30 = bf16[2,24,6272]{2,1,0:T(8,128)(2,1)S(1)} collective-permute-done((bf16[2,24,6272]{2,1,0:T(8,128)(2,1)S(1)}, bf16[2,24,6272]{2,1,0:T(8,128)(2,1)S(1)}, u32[]{:S(2)}, u32[]{:S(2)}) %collective-permute-start.30) | collective-permute-done | bytes 602144 | tf_op jit(solution)/shard_map/ppermute | solution.py:368
  520.2 26.3 %collective-permute-done.31 = bf16[2,2,24,6272]{3,2,0,1:T(8,128)(2,1)S(1)} collective-permute-done((bf16[2,2,24,6272]{3,2,0,1:T(8,128)(2,1)S(1)}, bf16[2,2,24,6272]{3,2,0,1:T(8,128)(2,1)S(1)}, u32[]{:S(2)}, u32[]{:S(2)}) %collective-permute-start.31) | collective-permute-done | bytes 1204256 | tf_op jit(solution)/shard_map/ppermute | solution.py:368
  (372 shorter events, 185.9 us)
Async XLA Ops:
  7.2 85.7 %all-gather.6.cloned.1.call-start = ((), (), s32[]{:S(2)}) async-start(), calls=%async_computation.3 | async-start | bytes 5308416 | tf_op jit(solution)/shard_map/all_gather | solution.py:555
  9.2 420.3 %reduce-scatter.2.cloned.1.call-start = ((), (), s32[]{:S(2)}) async-start(), calls=%async_computation.1 | async-start | bytes 2654208 | tf_op jit(solution)/shard_map/reduce_scatter | solution.py:655
  9.2 29.3 %collective-permute-start.3 = (bf16[192,3072]{1,0:T(8,128)(2,1)}, bf16[192,3072]{1,0:T(8,128)(2,1)S(1)}, u32[]{:S(2)}, u32[]{:S(2)}) collective-permute-start(bf16[192,3072]{1,0:T(8,128)(2,1)} %refs_0_), channel_id=1, source_target_pairs={{0,2},{1,3},{2,0},{3,1},{4,6},{5,7},{6,4},{7,5},{8,10},{9,11},{10,... | collective-permute-start | bytes 3538952 | tf_op jit(solution)/shard_map/ppermute | solution.py:368
  13.9 24.6 %collective-permute-start = (bf16[1,672]{1,0:T(2,128)(2,1)S(1)}, bf16[1,672]{1,0:T(2,128)(2,1)S(1)}, u32[]{:S(2)}, u32[]{:S(2)}) collective-permute-start(bf16[1,672]{1,0:T(2,128)(2,1)S(1)} %pad_maximum_fusion.4), channel_id=1, source_target_pairs={{0,2},{1,3},{2,0},{3,1},{4,6},{5,7},{6,4},{7,5},{8,10},{9,11},{10,... | collective-permute-start | bytes 4040 | tf_op jit(solution)/shard_map/ppermute | solution.py:368
  38.5 4.0 collective-permute-start.4
  38.5 4.7 collective-permute-start.5
  43.2 28.3 %collective-permute-start.6 = (bf16[192,3072]{1,0:T(8,128)(2,1)}, bf16[192,3072]{1,0:T(8,128)(2,1)}, u32[]{:S(2)}, u32[]{:S(2)}) collective-permute-start(bf16[192,3072]{1,0:T(8,128)(2,1)} %refs_0_.1), channel_id=1, source_target_pairs={{0,2},{1,3},{2,0},{3,1},{4,6},{5,7},{6,4},{7,5},{8,10},{9,11},{10,... | collective-permute-start | bytes 3538952 | tf_op jit(solution)/shard_map/ppermute | solution.py:368
  62.2 14.5 %collective-permute-start.7 = (bf16[192,3072]{1,0:T(8,128)(2,1)S(1)}, bf16[192,3072]{1,0:T(8,128)(2,1)}, u32[]{:S(2)}, u32[]{:S(2)}) collective-permute-start(bf16[192,3072]{1,0:T(8,128)(2,1)S(1)} %copy-done.36), channel_id=1, source_target_pairs={{0,1},{1,0},{2,3},{3,2},{4,5},{5,4},{6,7},{7,6},{8,9},{9,8},{10,11... | collective-permute-start | bytes 3538952 | tf_op jit(solution)/shard_map/ppermute | solution.py:368
  71.5 5.3 collective-permute-start.8
  72.3 63.5 %collective-permute-start.9 = (bf16[192,6144]{1,0:T(8,128)(2,1)}, bf16[192,6144]{1,0:T(8,128)(2,1)}, u32[]{:S(2)}, u32[]{:S(2)}) collective-permute-start(bf16[192,6144]{1,0:T(8,128)(2,1)} %refs_0_.2), channel_id=1, source_target_pairs={{0,2},{1,3},{2,0},{3,1},{4,6},{5,7},{6,4},{7,5},{8,10},{9,11},{10,... | collective-permute-start | bytes 7077896 | tf_op jit(solution)/shard_map/ppermute | solution.py:368
  135.7 25.0 %collective-permute-start.10 = (bf16[192,6144]{1,0:T(8,128)(2,1)}, bf16[192,6144]{1,0:T(8,128)(2,1)}, u32[]{:S(2)}, u32[]{:S(2)}) collective-permute-start(bf16[192,6144]{1,0:T(8,128)(2,1)} %refs_0_.2), channel_id=1, source_target_pairs={{0,1},{1,0},{2,3},{3,2},{4,5},{5,4},{6,7},{7,6},{8,9},{9,8},{10,11... | collective-permute-start | bytes 7077896 | tf_op jit(solution)/shard_map/ppermute | solution.py:368
  135.8 24.9 %collective-permute-start.11 = (bf16[192,6144]{1,0:T(8,128)(2,1)}, bf16[192,6144]{1,0:T(8,128)(2,1)}, u32[]{:S(2)}, u32[]{:S(2)}) collective-permute-start(bf16[192,6144]{1,0:T(8,128)(2,1)} %collective-permute-done.9.refs_1_), channel_id=1, source_target_pairs={{0,1},{1,0},{2,3},{3,2},{4,5},{5,4},{6,7},{7,6},{8,9},{9,8},{10,11... | collective-permute-start | bytes 7077896 | tf_op jit(solution)/shard_map/ppermute | solution.py:368
  184.3 30.4 %collective-permute-start.12 = (bf16[2,192,6144]{2,1,0:T(8,128)(2,1)}, bf16[2,192,6144]{2,1,0:T(8,128)(2,1)}, u32[]{:S(2)}, u32[]{:S(2)}) collective-permute-start(bf16[2,192,6144]{2,1,0:T(8,128)(2,1)} %pad_maximum_fusion), channel_id=1, source_target_pairs={{0,1},{1,0},{2,3},{3,2},{4,5},{5,4},{6,7},{7,6},{8,9},{9,8},{10,11... | collective-permute-start | bytes 14155784 | tf_op jit(solution)/shard_map/ppermute | solution.py:368
  241.6 53.9 %collective-permute-start.14 = (bf16[192,6144]{1,0:T(8,128)(2,1)}, bf16[192,6144]{1,0:T(8,128)(2,1)}, u32[]{:S(2)}, u32[]{:S(2)}) collective-permute-start(bf16[192,6144]{1,0:T(8,128)(2,1)} %fusion.8), channel_id=1, source_target_pairs={{0,2},{1,3},{2,0},{3,1},{4,6},{5,7},{6,4},{7,5},{8,10},{9,11},{10,... | collective-permute-start | bytes 7077896 | tf_op jit(solution)/shard_map/ppermute | solution.py:368
  247.3 53.0 %collective-permute-start.13 = (bf16[2,192,3072]{2,1,0:T(8,128)(2,1)}, bf16[2,192,3072]{2,1,0:T(8,128)(2,1)}, u32[]{:S(2)}, u32[]{:S(2)}) collective-permute-start(bf16[2,192,3072]{2,1,0:T(8,128)(2,1)} %pad_maximum_fusion.1), channel_id=1, source_target_pairs={{0,1},{1,0},{2,3},{3,2},{4,5},{5,4},{6,7},{7,6},{8,9},{9,8},{10,11... | collective-permute-start | bytes 7077896 | tf_op jit(solution)/shard_map/ppermute | solution.py:368
  253.5 60.0 %collective-permute-start.15 = (bf16[2,2,128,768]{3,2,0,1:T(8,128)(2,1)}, bf16[2,2,128,768]{3,2,0,1:T(8,128)(2,1)}, u32[]{:S(2)}, u32[]{:S(2)}) collective-permute-start(bf16[2,2,128,768]{3,2,0,1:T(8,128)(2,1)} %bitcast.329), channel_id=1, source_target_pairs={{0,4},{4,0},{8,12},{12,8},{16,20},{20,16},{24,28},{28,24},{1,5},{5... | collective-permute-start | bytes 2359304 | tf_op jit(solution)/shard_map/ppermute | solution.py:368
  315.5 27.9 %collective-permute-start.17 = (bf16[192,3072]{1,0:T(8,128)(2,1)}, bf16[192,3072]{1,0:T(8,128)(2,1)}, u32[]{:S(2)}, u32[]{:S(2)}) collective-permute-start(bf16[192,3072]{1,0:T(8,128)(2,1)} %fusion.48), channel_id=1, source_target_pairs={{0,2},{1,3},{2,0},{3,1},{4,6},{5,7},{6,4},{7,5},{8,10},{9,11},{10,... | collective-permute-start | bytes 3538952 | tf_op jit(solution)/shard_map/ppermute | solution.py:368
  317.0 29.6 %collective-permute-start.18 = (bf16[2,192,3072]{2,1,0:T(8,128)(2,1)}, bf16[2,192,3072]{2,1,0:T(8,128)(2,1)}, u32[]{:S(2)}, u32[]{:S(2)}) collective-permute-start(bf16[2,192,3072]{2,1,0:T(8,128)(2,1)} %pad_maximum_fusion.2), channel_id=1, source_target_pairs={{0,1},{1,0},{2,3},{3,2},{4,5},{5,4},{6,7},{7,6},{8,9},{9,8},{10,11... | collective-permute-start | bytes 7077896 | tf_op jit(solution)/shard_map/ppermute | solution.py:368
  326.3 11.7 %collective-permute-start.22 = (bf16[2,128,768]{2,1,0:T(8,128)(2,1)}, bf16[2,128,768]{2,1,0:T(8,128)(2,1)S(1)}, u32[]{:S(2)}, u32[]{:S(2)}) collective-permute-start(bf16[2,128,768]{2,1,0:T(8,128)(2,1)} %dynamic-slice_bitcast_fusion.4), channel_id=1, source_target_pairs={{0,8},{4,12},{8,0},{12,4},{16,24},{20,28},{24,16},{28,20},{1,9},{5... | collective-permute-start | bytes 1179656 | tf_op jit(solution)/shard_map/ppermute | solution.py:368
  330.7 221.3 %all-gather.4.cloned.1.call-start = ((), (), s32[]{:S(2)}) async-start(), calls=%async_computation.2 | async-start | bytes 2654208 | tf_op jit(solution)/shard_map/all_gather | solution.py:699
  331.0 47.8 %collective-permute-start.16 = (bf16[2,2,256,768]{3,2,0,1:T(8,128)(2,1)}, bf16[2,2,256,768]{3,2,0,1:T(8,128)(2,1)}, u32[]{:S(2)}, u32[]{:S(2)}) collective-permute-start(bf16[2,2,256,768]{3,2,0,1:T(8,128)(2,1)} %bitcast.359), channel_id=1, source_target_pairs={{0,4},{4,0},{8,12},{12,8},{16,20},{20,16},{24,28},{28,24},{1,5},{5... | collective-permute-start | bytes 4718600 | tf_op jit(solution)/shard_map/ppermute | solution.py:368
  348.3 36.4 %collective-permute-start.19 = (bf16[192,3072]{1,0:T(8,128)(2,1)S(1)}, bf16[192,3072]{1,0:T(8,128)(2,1)}, u32[]{:S(2)}, u32[]{:S(2)}) collective-permute-start(bf16[192,3072]{1,0:T(8,128)(2,1)S(1)} %fusion.53), channel_id=1, source_target_pairs={{0,2},{1,3},{2,0},{3,1},{4,6},{5,7},{6,4},{7,5},{8,10},{9,11},{10,... | collective-permute-start | bytes 3538952 | tf_op jit(solution)/shard_map/ppermute | solution.py:368
  353.8 26.9 %collective-permute-start.20 = (f32[32,12]{1,0:T(8,128)S(1)}, f32[32,12]{1,0:T(8,128)S(1)}, u32[]{:S(2)}, u32[]{:S(2)}) collective-permute-start(f32[32,12]{1,0:T(8,128)S(1)} %fusion.178), channel_id=1, source_target_pairs={{0,1},{1,0},{2,3},{3,2},{4,5},{5,4},{6,7},{7,6},{8,9},{9,8},{10,11... | collective-permute-start | bytes 4616 | tf_op jit(solution)/shard_map/ppermute | solution.py:368
  388.2 33.8 %collective-permute-start.24 = (bf16[2,2,24,6272]{3,2,1,0:T(8,128)(2,1)}, bf16[2,2,24,6272]{3,2,1,0:T(8,128)(2,1)}, u32[]{:S(2)}, u32[]{:S(2)}) collective-permute-start(bf16[2,2,24,6272]{3,2,1,0:T(8,128)(2,1)} %dynamic-slice_bitcast_fusion), channel_id=1, source_target_pairs={{0,4},{4,0},{8,12},{12,8},{16,20},{20,16},{24,28},{28,24},{1,5},{5... | collective-permute-start | bytes 3612680 | tf_op jit(solution)/shard_map/ppermute | solution.py:368
  388.2 31.2 %collective-permute-start.23 = (bf16[2,256,768]{2,1,0:T(8,128)(2,1)}, bf16[2,256,768]{2,1,0:T(8,128)(2,1)}, u32[]{:S(2)}, u32[]{:S(2)}) collective-permute-start(bf16[2,256,768]{2,1,0:T(8,128)(2,1)} %dynamic-slice_bitcast_fusion.1), channel_id=1, source_target_pairs={{0,8},{4,12},{8,0},{12,4},{16,24},{20,28},{24,16},{28,20},{1,9},{5... | collective-permute-start | bytes 2359304 | tf_op jit(solution)/shard_map/ppermute | solution.py:368
  390.7 38.0 %collective-permute-start.26 = (bf16[128,768]{1,0:T(8,128)(2,1)}, bf16[128,768]{1,0:T(8,128)(2,1)S(1)}, u32[]{:S(2)}, u32[]{:S(2)}) collective-permute-start(bf16[128,768]{1,0:T(8,128)(2,1)} %dynamic-slice_bitcast_fusion.6), channel_id=1, source_target_pairs={{0,16},{4,20},{8,24},{12,28},{16,0},{20,4},{24,8},{28,12},{1,17},{... | collective-permute-start | bytes 589832 | tf_op jit(solution)/shard_map/ppermute | solution.py:368
  424.8 26.2 %collective-permute-start.27 = (bf16[2,24,6272]{2,1,0:T(8,128)(2,1)S(1)}, bf16[2,24,6272]{2,1,0:T(8,128)(2,1)}, u32[]{:S(2)}, u32[]{:S(2)}) collective-permute-start(bf16[2,24,6272]{2,1,0:T(8,128)(2,1)S(1)} %dynamic-slice_bitcast_fusion.2), channel_id=1, source_target_pairs={{0,8},{4,12},{8,0},{12,4},{16,24},{20,28},{24,16},{28,20},{1,9},{5... | collective-permute-start | bytes 1806344 | tf_op jit(solution)/shard_map/ppermute | solution.py:368
  429.5 23.3 %collective-permute-start.25 = (bf16[256,768]{1,0:T(8,128)(2,1)}, bf16[256,768]{1,0:T(8,128)(2,1)S(1)}, u32[]{:S(2)}, u32[]{:S(2)}) collective-permute-start(bf16[256,768]{1,0:T(8,128)(2,1)} %dynamic-slice_bitcast_fusion.3), channel_id=1, source_target_pairs={{0,16},{4,20},{8,24},{12,28},{16,0},{20,4},{24,8},{28,12},{1,17},{... | collective-permute-start | bytes 1179656 | tf_op jit(solution)/shard_map/ppermute | solution.py:368
  452.2 18.7 %collective-permute-start.28 = (bf16[24,6272]{1,0:T(8,128)(2,1)S(1)}, bf16[24,6272]{1,0:T(8,128)(2,1)S(1)}, u32[]{:S(2)}, u32[]{:S(2)}) collective-permute-start(bf16[24,6272]{1,0:T(8,128)(2,1)S(1)} %dynamic-slice_bitcast_fusion.5), channel_id=1, source_target_pairs={{0,16},{4,20},{8,24},{12,28},{16,0},{20,4},{24,8},{28,12},{1,17},{... | collective-permute-start | bytes 903176 | tf_op jit(solution)/shard_map/ppermute | solution.py:368
  471.0 28.8 %collective-permute-start.29 = (bf16[24,6272]{1,0:T(8,128)(2,1)S(1)}, bf16[24,6272]{1,0:T(8,128)(2,1)S(1)}, u32[]{:S(2)}, u32[]{:S(2)}) collective-permute-start(bf16[24,6272]{1,0:T(8,128)(2,1)S(1)} %fusion.158), channel_id=1, source_target_pairs={{0,16},{4,20},{8,24},{12,28},{16,0},{20,4},{24,8},{28,12},{1,17},{... | collective-permute-start | bytes 903176 | tf_op jit(solution)/shard_map/ppermute | solution.py:368
  500.1 16.6 %collective-permute-start.30 = (bf16[2,24,6272]{2,1,0:T(8,128)(2,1)S(1)}, bf16[2,24,6272]{2,1,0:T(8,128)(2,1)S(1)}, u32[]{:S(2)}, u32[]{:S(2)}) collective-permute-start(bf16[2,24,6272]{2,1,0:T(8,128)(2,1)S(1)} %maximum_select_fusion.4), channel_id=1, source_target_pairs={{0,8},{4,12},{8,0},{12,4},{16,24},{20,28},{24,16},{28,20},{1,9},{5... | collective-permute-start | bytes 1806344 | tf_op jit(solution)/shard_map/ppermute | solution.py:368
  516.9 29.5 %collective-permute-start.31 = (bf16[2,2,24,6272]{3,2,0,1:T(8,128)(2,1)S(1)}, bf16[2,2,24,6272]{3,2,0,1:T(8,128)(2,1)S(1)}, u32[]{:S(2)}, u32[]{:S(2)}) collective-permute-start(bf16[2,2,24,6272]{3,2,0,1:T(8,128)(2,1)S(1)} %maximum_select_fusion.2), channel_id=1, source_target_pairs={{0,4},{4,0},{8,12},{12,8},{16,20},{20,16},{24,28},{28,24},{1,5},{5... | collective-permute-start | bytes 3612680 | tf_op jit(solution)/shard_map/ppermute | solution.py:368
  (82 other events, 630.8 us)
Sparse Core Ops, SparseCore 0:
  10.2 82.6 all-gather.5
  330.8 81.5 reduce-scatter.1
  429.7 75.3 all-gather.3
